TPU v7x, 512 devices: a whole 4x8x8 slice. The times are simulated.
512 devices in a mesh: rows: 32 (over x, z), cols: 16 (over y, core).
Axes of the slice: x: 4, y: 8, z: 8, core: 2. Of those that a mesh axis runs over, the one named last changes fastest.
Arguments:
- features: bfloat16 [512, 256, 256], P('rows', 'cols'), may hold values from -6 to 6
- conv_weight: bfloat16 [4, 4, 256, 256], replicated, may hold values from -0.1875 to 0.1875
- query_weight: bfloat16 [256, 256], replicated, may hold values from -0.375 to 0.375
- kv_weight: bfloat16 [256, 512], replicated, may hold values from -0.375 to 0.375
- out_weight: bfloat16 [256, 256], replicated, may hold values from -0.375 to 0.375
- queries: float32 [100, 256], replicated, may hold values from -150 to 150
- norm_gain: float32 [256], replicated, may hold values from 0.5 to 1.5
- active_blocks: int32 [100, 32], replicated, may hold values from 0 to 511, all different within a row
Outputs:
- pixels: bfloat16 [1024, 512, 256], P('rows', 'cols')
- attended: float32 [100, 256], replicated
- updated: float32 [100, 256], replicated
Inputs may be any that keep to these rules, and one draw needn't show every extreme that they name: `active_blocks`: each query names 32 different blocks of 32 x 32 pixels; every block is named by some query.
All inputs are finite; a program needn't handle non-finite values.
Results may differ from a plain program's by a relative error of at most 0.0045.
The roundings to bfloat16 on the way count: a program that leaves them out, or rounds other values in their place, can miss the bound.
Values may be sent and summed in bfloat16 or wider, within the bound.
No kernel may reach another device: no remote copies, remote signals or barrier semaphores. Data moves between devices by JAX's collectives and lax.ppermute only.
A program may use at most 128 MiB of HBM per device.

v0:
```python
import functools

import jax
import jax.numpy as jnp
from jax import lax
from jax.experimental import pallas as pl
from jax.experimental.pallas import tpu as pltpu
from jax.sharding import PartitionSpec as P

QUERIES = 100
PADDED = 104
HEADS = 8
HEAD = 32
BLOCK = 32
C = 256
LANES = 128
ROWS_IN = 16
COLS_IN = 16
LIST = 32
PAYLOAD = C + LANES

masked_low = -1e30
tap_table = (((1, 1), (0, 3)), ((1, 2), (2, 0)))
query_chunks = ((0, 40), (40, 32), (72, 32))


def dot(a, b):
    return jnp.dot(a, b, preferred_element_type=jnp.float32)


def dot_exact(a, b):
    return jnp.dot(a, b, preferred_element_type=jnp.float32, precision=lax.Precision.HIGHEST)


def iota(shape, dim):
    return lax.broadcasted_iota(jnp.int32, shape, dim)


def local_kernel(
    x_ref, top_ref, bottom_ref, left_ref, right_ref, weight_ref, query_weight_ref, kv_weight_ref,
    queries_ref, active_blocks_ref, pixels_ref, part_ref, shifted, joined, wide_queries, keys, values, flags, spread
):
    height = ROWS_IN + 2
    middle = jnp.concatenate([top_ref[...], x_ref[...], bottom_ref[...]], axis=0)
    shifted[1] = middle.reshape(height * COLS_IN, C)
    middle = middle.astype(jnp.float32)
    column = iota((height, COLS_IN, C), 1)
    left = left_ref[...].astype(jnp.float32)
    right = right_ref[...].astype(jnp.float32)
    before = jnp.where(column == 0, left, pltpu.roll(middle, 1, 1))
    after = jnp.where(column == COLS_IN - 1, right, pltpu.roll(middle, COLS_IN - 1, 1))
    shifted[0] = before.astype(jnp.bfloat16).reshape(height * COLS_IN, C)
    shifted[2] = after.astype(jnp.bfloat16).reshape(height * COLS_IN, C)

    area = ROWS_IN * COLS_IN
    for a in range(2):
        for b in range(2):
            total = None
            for row_offset, row_kernel in tap_table[a]:
                for col_offset, col_kernel in tap_table[b]:
                    window = shifted[col_offset, row_offset * COLS_IN : row_offset * COLS_IN + area]
                    term = dot(window, weight_ref[row_kernel, col_kernel])
                    total = term if total is None else total + term
            for half in range(2):
                part = total[:, half * LANES : (half + 1) * LANES].reshape(ROWS_IN, COLS_IN, LANES)
                joined[half, :, a, pl.ds(b, COLS_IN, stride=2), :] = part
            key_value = dot(total.astype(jnp.bfloat16), kv_weight_ref[...]).astype(jnp.bfloat16)
            at = (2 * a + b) * area
            keys[at : at + area] = key_value[:, :C]
            values[at : at + area] = key_value[:, C:]
    for half in range(2):
        part = joined[half].reshape(2 * ROWS_IN, 2 * COLS_IN, LANES).astype(jnp.bfloat16)
        pixels_ref[:, :, half * LANES : (half + 1) * LANES] = part

    projected = dot(queries_ref[...].astype(jnp.bfloat16), query_weight_ref[...]) * HEAD ** (-0.5)
    spread[:QUERIES] = projected
    spread[QUERIES:] = jnp.zeros((PADDED - QUERIES, C), jnp.float32)
    own_head = iota((1, HEADS, C), 2) // HEAD == iota((1, HEADS, C), 1)
    each = jnp.where(own_head, spread[...][:, None, :], 0.0)
    wide_queries[...] = each.reshape(PADDED * HEADS, C).astype(jnp.bfloat16)

    block_id = lax.axis_index("rows") * lax.axis_size("cols") + lax.axis_index("cols")
    hits = (active_blocks_ref[...] == block_id).astype(jnp.float32)
    flags[:QUERIES] = jnp.broadcast_to(jnp.max(hits, axis=1, keepdims=True), (QUERIES, LANES))
    flags[QUERIES:] = jnp.zeros((PADDED - QUERIES, LANES), jnp.float32)
    lane = iota((1, HEADS, LANES), 2)
    head = iota((1, HEADS, LANES), 1)
    ones = jnp.ones((4 * area, LANES), jnp.bfloat16)
    for start, count in query_chunks:
        rows = slice(start * HEADS, (start + count) * HEADS)
        now = lax.dot_general(
            wide_queries[rows], keys[...], (((1,), (1,)), ((), ())), preferred_element_type=jnp.float32
        )
        highest = jnp.max(now, axis=1, keepdims=True)
        weights = jnp.exp(now - highest).astype(jnp.bfloat16)
        summed = dot(weights, values[...]).reshape(count, HEADS, C)
        totals = dot(weights, ones).reshape(count, HEADS, LANES)
        highest = jnp.broadcast_to(highest, (count * HEADS, LANES)).reshape(count, HEADS, LANES)
        here = flags[start : start + count] > 0.0
        summed = jnp.sum(jnp.where(own_head, summed, 0.0), axis=1)
        part_ref[start : start + count, :C] = jnp.where(here[:, :1], summed, 0.0)
        totals = jnp.sum(jnp.where(lane == head + HEADS, totals, 0.0), axis=1)
        highest = jnp.sum(jnp.where(lane == head, highest, 0.0), axis=1)
        low = jnp.where(iota((count, LANES), 1) < HEADS, masked_low, 0.0)
        part_ref[start : start + count, C:] = jnp.where(here, totals + highest, low)


def local(x, top, bottom, left, right, weight, query_weight, kv_weight, queries, active_blocks):
    area = ROWS_IN * COLS_IN
    return pl.pallas_call(
        local_kernel,
        out_shape=(
            jax.ShapeDtypeStruct((2 * ROWS_IN, 2 * COLS_IN, C), jnp.bfloat16),
            jax.ShapeDtypeStruct((PADDED, PAYLOAD), jnp.float32),
        ),
        in_specs=[pl.BlockSpec(memory_space=pltpu.VMEM)] * 10,
        out_specs=[pl.BlockSpec(memory_space=pltpu.VMEM)] * 2,
        scratch_shapes=[
            pltpu.VMEM((3, (ROWS_IN + 2) * COLS_IN, C), jnp.bfloat16),
            pltpu.VMEM((2, ROWS_IN, 2, 2 * COLS_IN, LANES), jnp.float32),
            pltpu.VMEM((PADDED * HEADS, C), jnp.bfloat16),
            pltpu.VMEM((4 * area, C), jnp.bfloat16),
            pltpu.VMEM((4 * area, C), jnp.bfloat16),
            pltpu.VMEM((PADDED, LANES), jnp.float32),
            pltpu.VMEM((PADDED, C), jnp.float32),
        ],
        compiler_params=pltpu.CompilerParams(vmem_limit_bytes=40 << 20),
        cost_estimate=pl.CostEstimate(flops=2_000_000_000, bytes_accessed=4_000_000, transcendentals=800_000),
    )(x, top, bottom, left, right, weight, query_weight, kv_weight, queries, active_blocks)


def widening():
    return (iota((LANES, C), 1) // HEAD == iota((LANES, C), 0)).astype(jnp.float32)


def merge(parts):
    n, q, _ = parts.shape
    side = parts[:, :, C:]
    top = jnp.max(side, axis=0)
    is_max = iota((n, q, LANES), 2) < HEADS
    factor = jnp.where(is_max, jnp.exp(jnp.where(is_max, side - top[None], 0.0)), 0.0)
    wide = dot_exact(factor.reshape(n * q, LANES), widening()).reshape(n, q, C)
    summed = jnp.sum(parts[:, :, :C] * wide, axis=0)
    moved = pltpu.roll(factor.reshape(n * q, LANES), HEADS, 1).reshape(n, q, LANES)
    totals = jnp.sum(side * moved, axis=0)
    return summed, jnp.where(iota((q, LANES), 1) < HEADS, top, totals)


def merge_kernel(parts_ref, out_ref):
    summed, side = merge(parts_ref[...])
    out_ref[:, :, :C] = jnp.broadcast_to(summed[None], (out_ref.shape[0], *summed.shape))
    out_ref[:, :, C:] = jnp.broadcast_to(side[None], (out_ref.shape[0], *side.shape))


def attend_kernel(parts_ref, out_ref):
    summed, side = merge(parts_ref[...])
    q = side.shape[0]
    totals = pltpu.roll(side, LANES - HEADS, 1)
    totals = jnp.where(iota((q, LANES), 1) < HEADS, totals, 0.0)
    out_ref[...] = summed / dot_exact(totals, widening())


def finish_kernel(attention_ref, out_weight_ref, queries_ref, gain_ref, attended_ref, updated_ref):
    attention = attention_ref[...].reshape(-1, C)[:PADDED].astype(jnp.bfloat16)
    attended = dot(attention, out_weight_ref[...])[:QUERIES]
    attended_ref[...] = attended
    residual_sum = queries_ref[...] + attended
    average = jnp.mean(residual_sum, axis=1, keepdims=True)
    centred = residual_sum - average
    deviation = jnp.mean(centred * centred, axis=1, keepdims=True)
    updated_ref[...] = centred * lax.rsqrt(deviation + 1e-05) * gain_ref[...]


def on_device(kernel, out_shape, *operands):
    return pl.pallas_call(
        kernel,
        out_shape=out_shape,
        in_specs=[pl.BlockSpec(memory_space=pltpu.VMEM)] * len(operands),
        out_specs=jax.tree.map(lambda _: pl.BlockSpec(memory_space=pltpu.VMEM), out_shape),
        compiler_params=pltpu.CompilerParams(vmem_limit_bytes=32 << 20),
        cost_estimate=pl.CostEstimate(flops=10_000_000, bytes_accessed=500_000, transcendentals=10_000),
    )(*operands)


def neighbours(x, axis, dim):
    peers = lax.axis_size(axis)
    up = [(i, i + 1) for i in range(peers - 1)]
    down = [(j, i) for i, j in up]
    last = lax.slice_in_dim(x, x.shape[dim] - 1, x.shape[dim], axis=dim)
    first = lax.slice_in_dim(x, 0, 1, axis=dim)
    return lax.ppermute(last, axis, up), lax.ppermute(first, axis, down)


def body(
    features, conv_weight, query_weight, kv_weight, out_weight, queries, norm_gain, active_blocks
):
    top, bottom = neighbours(features, "rows", 0)
    edges = jnp.concatenate(
        [jnp.concatenate([part[:, :1], part[:, -1:]], axis=1) for part in (top, features, bottom)], axis=0
    )
    left, right = neighbours(edges, "cols", 1)
    pixels, part = local(
        features, top, bottom, left, right, conv_weight, query_weight, kv_weight, queries, active_blocks
    )
    peers = lax.axis_size("cols")
    share = 8
    part = jnp.pad(part, ((0, peers * share - PADDED), (0, 0))).reshape(peers, share, PAYLOAD)
    parts = lax.all_to_all(part, "cols", 0, 0)
    copies = jax.ShapeDtypeStruct((lax.axis_size("rows"), share, PAYLOAD), jnp.float32)
    parts = lax.all_to_all(on_device(merge_kernel, copies, parts), "rows", 0, 0)
    attention = on_device(attend_kernel, jax.ShapeDtypeStruct((share, C), jnp.float32), parts)
    attention = lax.all_gather(attention, "cols")
    out = jax.ShapeDtypeStruct((QUERIES, C), jnp.float32)
    attended, updated = on_device(
        finish_kernel, (out, out), attention, out_weight, queries, norm_gain.reshape(1, C)
    )
    return (pixels, attended, updated)


def solution(mesh):
    placed = (P("rows", "cols", None), P(), P(), P(), P(), P(), P(), P())
    return jax.shard_map(
        body,
        mesh=mesh,
        in_specs=placed,
        out_specs=(P("rows", "cols", None), P(), P()),
        check_vma=False,
    )
```

profile of v0, /device:TPU:1, one launch (start us, length us, event | category | flops | bytes accessed | tf_op | source)
XLA Modules:
  0.0 92.2 jit_solution(1744396150596581228)
XLA Ops:
  0.6 0.7 fusion.1
  1.4 1.3 %collective-permute-start.1 = (bf16[1,16,256]{2,1,0:T(8,128)(2,1)S(1)}, bf16[1,16,256]{2,1,0:T(8,128)(2,1)S(1)}, u32[]{:S(2)}, u32[]{:S(2)}) collective-permute-start(bf16[1,16,256]{2,1,0:T(8,128)(2,1)S(1)} %get-tuple-element.13), channel_id=1, source_target_pairs={{16,0},{32,16},{48,32},{64,48},{80,64},{96,80},{112,96},{128,112},... | collective-permute-start | bytes 24584 | tf_op jit(solution)/shard_map/ppermute | solution.py:191
  2.6 5.5 %collective-permute-start = (bf16[1,16,256]{2,1,0:T(8,128)(2,1)S(1)}, bf16[1,16,256]{2,1,0:T(8,128)(2,1)S(1)}, u32[]{:S(2)}, u32[]{:S(2)}) collective-permute-start(bf16[1,16,256]{2,1,0:T(8,128)(2,1)S(1)} %get-tuple-element.14), channel_id=1, source_target_pairs={{0,16},{16,32},{32,48},{48,64},{64,80},{80,96},{96,112},{112,128},... | collective-permute-start | bytes 24584 | tf_op jit(solution)/shard_map/ppermute | solution.py:191
  8.1 0.9 fusion
  9.0 0.0 collective-permute-done.1.bottom_ref
  9.0 0.0 collective-permute-done.top_ref
  9.2 8.3 %collective-permute-start.3 = (bf16[18,1,256]{2,1,0:T(2,128)(2,1)S(1)}, bf16[18,1,256]{2,1,0:T(2,128)(2,1)S(1)}, u32[]{:S(2)}, u32[]{:S(2)}) collective-permute-start(bf16[18,1,256]{2,1,0:T(2,128)(2,1)S(1)} %get-tuple-element.15), channel_id=1, source_target_pairs={{1,0},{2,1},{3,2},{4,3},{5,4},{6,5},{7,6},{8,7},{9,8},{10,9},{11,1... | collective-permute-start | bytes 27656 | tf_op jit(solution)/shard_map/ppermute | solution.py:191
  17.4 1.9 %collective-permute-start.2 = (bf16[18,1,256]{2,1,0:T(2,128)(2,1)S(1)}, bf16[18,1,256]{2,1,0:T(2,128)(2,1)S(1)}, u32[]{:S(2)}, u32[]{:S(2)}) collective-permute-start(bf16[18,1,256]{2,1,0:T(2,128)(2,1)S(1)} %get-tuple-element.16), channel_id=1, source_target_pairs={{0,1},{1,2},{2,3},{3,4},{4,5},{5,6},{6,7},{7,8},{8,9},{9,10},{10,1... | collective-permute-start | bytes 27656 | tf_op jit(solution)/shard_map/ppermute | solution.py:191
  19.4 0.8 copy.11.active_blocks_ref
  20.2 0.0 collective-permute-done.3.right_ref
  20.2 0.3 collective-permute-done.2.left_ref
  20.5 0.0 copy-start.1
  20.5 0.9 copy-done.1
  21.4 0.0 copy-start.2
  21.4 0.9 copy-done.2
  22.3 0.0 copy-start.4
  22.3 1.6 %copy-done.4 = bf16[4,4,256,256]{3,2,1,0:T(8,128)(2,1)S(1)} copy-done((bf16[4,4,256,256]{3,2,1,0:T(8,128)(2,1)S(1)}, bf16[4,4,256,256]{3,2,1,0:T(8,128)(2,1)}, u32[]{:S(2)}) %copy-start.4) | copy-done | bytes 2097176
  23.9 0.0 copy-start.5
  23.9 0.9 %copy-done.5 = bf16[256,512]{1,0:T(8,128)(2,1)S(1)} copy-done((bf16[256,512]{1,0:T(8,128)(2,1)S(1)}, bf16[256,512]{1,0:T(8,128)(2,1)}, u32[]{:S(2)}) %copy-start.5) | copy-done | bytes 262168
  24.9 0.0 copy-start.6
  24.9 0.9 copy-done.6
  25.8 4.4 %shard_map.103 = (bf16[32,32,256]{2,1,0:T(8,128)(2,1)}, f32[104,384]{1,0:T(8,128)S(1)}) custom-call(bf16[16,16,256]{2,1,0:T(8,128)(2,1)S(1)} %copy-done.2, bf16[1,16,256]{2,1,0:T(8,128)(2,1)S(1)} %collective-permute-done.top_ref, bf16[1,16,256]{2,1,0:T(8,128)(2,1)S(1)} %collective-permute-done.1.bottom_ref, ...), custom_call_target="tpu_custom_call" | custom-call | flops 2000000000 | bytes 4000000 | tf_op jit(solution)/shard_map/pallas_call | solution.py:110
  30.2 0.0 copy-start
  30.2 0.0 copy-start.3
  30.2 15.6 %all_to_all.10.parts_ref = f32[16,8,384]{2,1,0:T(8,128)S(1)} all-to-all(f32[16,8,384]{2,1,0:T(8,128)S(1)} %pad_bitcast_fusion), channel_id=1, replica_groups=mesh['rows'=32,'cols'=16] {'cols'}, dimensions={0} | all-to-all | bytes 393216 | tf_op jit(solution)/shard_map/all_to_all | solution.py:208
  45.8 0.3 shard_map.104
  46.0 28.4 %all_to_all.11.parts_ref = f32[32,8,384]{2,1,0:T(8,128)S(1)} all-to-all(f32[32,8,384]{2,1,0:T(8,128)S(1)} %shard_map.104), channel_id=1, replica_groups=mesh['rows'=32,'cols'=16] {'rows'}, dimensions={0} | all-to-all | bytes 786432 | tf_op jit(solution)/shard_map/all_to_all | solution.py:210
  74.5 0.4 shard_map.105
  74.9 16.3 %all-gather = f32[128,256]{1,0:T(8,128)S(1)} all-gather(f32[8,256]{1,0:T(8,128)S(1)} %shard_map.105), channel_id=2, replica_groups=mesh['rows'=32,'cols'=16] {'cols'}, dimensions={0}, use_global_device_ids=true | all-gather | bytes 139264 | tf_op jit(solution)/shard_map/all_gather | solution.py:212
  91.2 0.0 copy-done
  91.2 0.0 copy-done.3
  91.2 1.0 %shard_map.106 = (f32[100,256]{1,0:T(8,128)}, f32[100,256]{1,0:T(8,128)}) custom-call(f32[16,8,256]{2,1,0:T(8,128)S(1)} %bitcast.4, bf16[256,256]{1,0:T(8,128)(2,1)S(1)} %copy-done, f32[100,256]{1,0:T(8,128)S(1)} %copy-done.1, f32[1,256]{1,0:T(1,128)S(1)} %bitcast.5), custom_call_target="tpu_custom_call" | custom-call | flops 10000000 | bytes 500000 | tf_op jit(solution)/shard_map/pallas_call | solution.py:175
  (5 shorter events, 0.1 us)
Async XLA Ops:
  1.4 7.7 %collective-permute-start.1 = (bf16[1,16,256]{2,1,0:T(8,128)(2,1)S(1)}, bf16[1,16,256]{2,1,0:T(8,128)(2,1)S(1)}, u32[]{:S(2)}, u32[]{:S(2)}) collective-permute-start(bf16[1,16,256]{2,1,0:T(8,128)(2,1)S(1)} %get-tuple-element.13), channel_id=1, source_target_pairs={{16,0},{32,16},{48,32},{64,48},{80,64},{96,80},{112,96},{128,112},... | collective-permute-start | bytes 24584 | tf_op jit(solution)/shard_map/ppermute | solution.py:191
  2.6 6.4 %collective-permute-start = (bf16[1,16,256]{2,1,0:T(8,128)(2,1)S(1)}, bf16[1,16,256]{2,1,0:T(8,128)(2,1)S(1)}, u32[]{:S(2)}, u32[]{:S(2)}) collective-permute-start(bf16[1,16,256]{2,1,0:T(8,128)(2,1)S(1)} %get-tuple-element.14), channel_id=1, source_target_pairs={{0,16},{16,32},{32,48},{48,64},{64,80},{80,96},{96,112},{112,128},... | collective-permute-start | bytes 24584 | tf_op jit(solution)/shard_map/ppermute | solution.py:191
  9.2 11.0 %collective-permute-start.3 = (bf16[18,1,256]{2,1,0:T(2,128)(2,1)S(1)}, bf16[18,1,256]{2,1,0:T(2,128)(2,1)S(1)}, u32[]{:S(2)}, u32[]{:S(2)}) collective-permute-start(bf16[18,1,256]{2,1,0:T(2,128)(2,1)S(1)} %get-tuple-element.15), channel_id=1, source_target_pairs={{1,0},{2,1},{3,2},{4,3},{5,4},{6,5},{7,6},{8,7},{9,8},{10,9},{11,1... | collective-permute-start | bytes 27656 | tf_op jit(solution)/shard_map/ppermute | solution.py:191
  17.4 3.1 %collective-permute-start.2 = (bf16[18,1,256]{2,1,0:T(2,128)(2,1)S(1)}, bf16[18,1,256]{2,1,0:T(2,128)(2,1)S(1)}, u32[]{:S(2)}, u32[]{:S(2)}) collective-permute-start(bf16[18,1,256]{2,1,0:T(2,128)(2,1)S(1)} %get-tuple-element.16), channel_id=1, source_target_pairs={{0,1},{1,2},{2,3},{3,4},{4,5},{5,6},{6,7},{7,8},{8,9},{9,10},{10,1... | collective-permute-start | bytes 27656 | tf_op jit(solution)/shard_map/ppermute | solution.py:191
  20.5 0.9 copy-start.1
  21.4 0.9 copy-start.2
  22.3 1.6 %copy-start.4 = (bf16[4,4,256,256]{3,2,1,0:T(8,128)(2,1)S(1)}, bf16[4,4,256,256]{3,2,1,0:T(8,128)(2,1)}, u32[]{:S(2)}) copy-start(bf16[4,4,256,256]{3,2,1,0:T(8,128)(2,1)} %weight_ref.1) | copy-start | bytes 6291460
  23.9 0.9 %copy-start.5 = (bf16[256,512]{1,0:T(8,128)(2,1)S(1)}, bf16[256,512]{1,0:T(8,128)(2,1)}, u32[]{:S(2)}) copy-start(bf16[256,512]{1,0:T(8,128)(2,1)} %kv_weight_ref.1) | copy-start | bytes 786436
  24.9 0.9 copy-start.6
  30.2 61.1 %copy-start = (bf16[256,256]{1,0:T(8,128)(2,1)S(1)}, bf16[256,256]{1,0:T(8,128)(2,1)}, u32[]{:S(2)}) copy-start(bf16[256,256]{1,0:T(8,128)(2,1)} %out_weight_ref.1) | copy-start | bytes 393220
  30.2 61.1 %copy-start.3 = (f32[256]{0:T(256)S(1)}, f32[256]{0:T(256)}, u32[]{:S(2)}) copy-start(f32[256]{0:T(256)} %param.14) | copy-start | bytes 3076
where the time goes:
time: 92.8 us; the launch traced here: 92.2 us
  blocking collectives  60.3 us (65%)
  starting transfers between devices  16.9 us (18%)
  local copies, waits for them, and re-layouts  7.76 us (8%)
  Pallas kernels  6.09 us (7%)
    all_to_all x1, blocking collectives, body(): parts = lax.all_to_all(on_device(merge_kernel, copies, parts), 'rows', 0, 0)  28.4 us
    ppermute x4, starting transfers between devices, neighbours(): return (lax.ppermute(last, axis, up), lax.ppermute(first, axis, down))  16.9 us
    all_gather x1, blocking collectives, body(): attention = lax.all_gather(attention, 'cols')  16.3 us
    all_to_all x1, blocking collectives, body(): parts = lax.all_to_all(part, 'cols', 0, 0)  15.6 us
    unnamed x15, local copies, waits for them, and re-layouts  6.07 us
    pallas_call x1, Pallas kernels, local(): pl.pallas_call(local_kernel, out_shape=(jax.ShapeDtypeStruct((2 * ROWS_IN...  4.4 us
  transfers between devices with their start and end apart: 4, of which 1 were waited for; matrix products, arithmetic and copies ran while one was open for 2% of the time, Pallas kernels for 0%

commit v1 on v0

--- a/solution.py
+++ b/solution.py
@@ -37,9 +37,47 @@
 
 
 def local_kernel(
-    x_ref, top_ref, bottom_ref, left_ref, right_ref, weight_ref, query_weight_ref, kv_weight_ref,
-    queries_ref, active_blocks_ref, pixels_ref, part_ref, shifted, joined, wide_queries, keys, values, flags, spread
+    x_hbm, top_ref, bottom_ref, left_ref, right_ref, weight_hbm, query_weight_hbm, kv_weight_hbm,
+    queries_hbm, named_hbm, pixels_hbm, part_ref,
+    x_ref, weight_ref, query_weight_ref, kv_weight_ref, queries_ref, named_ref, pixels_ref,
+    shifted, joined, wide_queries, keys, values, flags, spread, arrived, sent
 ):
+    def fetch(source, target, slot):
+        copy = pltpu.make_async_copy(source, target, arrived.at[slot])
+        copy.start()
+        return copy
+
+    fetch_queries = fetch(queries_hbm, queries_ref, 0)
+    fetch_query_weight = fetch(query_weight_hbm, query_weight_ref, 1)
+    fetch_named = fetch(named_hbm, named_ref, 2)
+    fetch_x = fetch(x_hbm, x_ref, 3)
+    fetch_weight = {}
+    for a in range(2):
+        for _, row_kernel in tap_table[a]:
+            fetch_weight[row_kernel] = fetch(
+                weight_hbm.at[row_kernel], weight_ref.at[row_kernel], 4 + row_kernel
+            )
+        if a == 0:
+            fetch_kv_weight = fetch(kv_weight_hbm, kv_weight_ref, 8)
+
+    own_head = iota((1, HEADS, C), 2) // HEAD == iota((1, HEADS, C), 1)
+    fetch_queries.wait()
+    fetch_query_weight.wait()
+    projected = dot(queries_ref[...].astype(jnp.bfloat16), query_weight_ref[...]) * HEAD ** (-0.5)
+    spread[:QUERIES] = projected
+    spread[QUERIES:] = jnp.zeros((PADDED - QUERIES, C), jnp.float32)
+    each = jnp.where(own_head, spread[...][:, None, :], 0.0)
+    wide_queries[...] = each.reshape(PADDED * HEADS, C).astype(jnp.bfloat16)
+
+    fetch_named.wait()
+    block_id = lax.axis_index("rows") * lax.axis_size("cols") + lax.axis_index("cols")
+    hits = (named_ref[...] == block_id).astype(jnp.bfloat16)
+    flags[:QUERIES] = lax.dot_general(
+        hits, jnp.ones((hits.shape[0], LANES), jnp.bfloat16), (((0,), (0,)), ((), ())), preferred_element_type=jnp.float32
+    )
+    flags[QUERIES:] = jnp.zeros((PADDED - QUERIES, LANES), jnp.float32)
+
+    fetch_x.wait()
     height = ROWS_IN + 2
     middle = jnp.concatenate([top_ref[...], x_ref[...], bottom_ref[...]], axis=0)
     shifted[1] = middle.reshape(height * COLS_IN, C)
@@ -54,6 +92,10 @@
 
     area = ROWS_IN * COLS_IN
     for a in range(2):
+        for _, row_kernel in tap_table[a]:
+            fetch_weight[row_kernel].wait()
+        if a == 0:
+            fetch_kv_weight.wait()
         for b in range(2):
             total = None
             for row_offset, row_kernel in tap_table[a]:
@@ -71,18 +113,9 @@
     for half in range(2):
         part = joined[half].reshape(2 * ROWS_IN, 2 * COLS_IN, LANES).astype(jnp.bfloat16)
         pixels_ref[:, :, half * LANES : (half + 1) * LANES] = part
-
-    projected = dot(queries_ref[...].astype(jnp.bfloat16), query_weight_ref[...]) * HEAD ** (-0.5)
-    spread[:QUERIES] = projected
-    spread[QUERIES:] = jnp.zeros((PADDED - QUERIES, C), jnp.float32)
-    own_head = iota((1, HEADS, C), 2) // HEAD == iota((1, HEADS, C), 1)
-    each = jnp.where(own_head, spread[...][:, None, :], 0.0)
-    wide_queries[...] = each.reshape(PADDED * HEADS, C).astype(jnp.bfloat16)
-
-    block_id = lax.axis_index("rows") * lax.axis_size("cols") + lax.axis_index("cols")
-    hits = (active_blocks_ref[...] == block_id).astype(jnp.float32)
-    flags[:QUERIES] = jnp.broadcast_to(jnp.max(hits, axis=1, keepdims=True), (QUERIES, LANES))
-    flags[QUERIES:] = jnp.zeros((PADDED - QUERIES, LANES), jnp.float32)
+    send_pixels = pltpu.make_async_copy(pixels_ref, pixels_hbm, sent)
+    send_pixels.start()
+
     lane = iota((1, HEADS, LANES), 2)
     head = iota((1, HEADS, LANES), 1)
     ones = jnp.ones((4 * area, LANES), jnp.bfloat16)
@@ -98,24 +131,32 @@
         highest = jnp.broadcast_to(highest, (count * HEADS, LANES)).reshape(count, HEADS, LANES)
         here = flags[start : start + count] > 0.0
         summed = jnp.sum(jnp.where(own_head, summed, 0.0), axis=1)
-        part_ref[start : start + count, :C] = jnp.where(here[:, :1], summed, 0.0)
+        share = part_ref.shape[1]
+        shares = slice(start // share, (start + count) // share)
+        part_ref[shares, :, :C] = jnp.where(here[:, :1], summed, 0.0).reshape(-1, share, C)
         totals = jnp.sum(jnp.where(lane == head + HEADS, totals, 0.0), axis=1)
         highest = jnp.sum(jnp.where(lane == head, highest, 0.0), axis=1)
         low = jnp.where(iota((count, LANES), 1) < HEADS, masked_low, 0.0)
-        part_ref[start : start + count, C:] = jnp.where(here, totals + highest, low)
-
-
-def local(x, top, bottom, left, right, weight, query_weight, kv_weight, queries, active_blocks):
+        part_ref[shares, :, C:] = jnp.where(here, totals + highest, low).reshape(-1, share, LANES)
+    filled = PADDED // share
+    if filled < part_ref.shape[0]:
+        part_ref[filled:] = jnp.zeros((part_ref.shape[0] - filled, share, PAYLOAD), jnp.float32)
+    send_pixels.wait()
+
+
+def local(x, top, bottom, left, right, weight, query_weight, kv_weight, queries, active_blocks, part_shape):
     area = ROWS_IN * COLS_IN
+    pixels = jax.ShapeDtypeStruct((2 * ROWS_IN, 2 * COLS_IN, C), jnp.bfloat16)
+    vmem = pl.BlockSpec(memory_space=pltpu.VMEM)
+    hbm = pl.BlockSpec(memory_space=pltpu.HBM)
+    named = active_blocks.T
     return pl.pallas_call(
         local_kernel,
-        out_shape=(
-            jax.ShapeDtypeStruct((2 * ROWS_IN, 2 * COLS_IN, C), jnp.bfloat16),
-            jax.ShapeDtypeStruct((PADDED, PAYLOAD), jnp.float32),
-        ),
-        in_specs=[pl.BlockSpec(memory_space=pltpu.VMEM)] * 10,
-        out_specs=[pl.BlockSpec(memory_space=pltpu.VMEM)] * 2,
-        scratch_shapes=[
+        out_shape=(pixels, jax.ShapeDtypeStruct(part_shape, jnp.float32)),
+        in_specs=[hbm] + [vmem] * 4 + [hbm] * 5,
+        out_specs=[hbm, vmem],
+        scratch_shapes=[pltpu.VMEM(t.shape, t.dtype) for t in (x, weight, query_weight, kv_weight, queries, named, pixels)]
+        + [
             pltpu.VMEM((3, (ROWS_IN + 2) * COLS_IN, C), jnp.bfloat16),
             pltpu.VMEM((2, ROWS_IN, 2, 2 * COLS_IN, LANES), jnp.float32),
             pltpu.VMEM((PADDED * HEADS, C), jnp.bfloat16),
@@ -123,10 +164,12 @@
             pltpu.VMEM((4 * area, C), jnp.bfloat16),
             pltpu.VMEM((PADDED, LANES), jnp.float32),
             pltpu.VMEM((PADDED, C), jnp.float32),
+            pltpu.SemaphoreType.DMA((9,)),
+            pltpu.SemaphoreType.DMA,
         ],
-        compiler_params=pltpu.CompilerParams(vmem_limit_bytes=40 << 20),
+        compiler_params=pltpu.CompilerParams(vmem_limit_bytes=60 << 20),
         cost_estimate=pl.CostEstimate(flops=2_000_000_000, bytes_accessed=4_000_000, transcendentals=800_000),
-    )(x, top, bottom, left, right, weight, query_weight, kv_weight, queries, active_blocks)
+    )(x, top, bottom, left, right, weight, query_weight, kv_weight, queries, named)
 
 
 def widening():
@@ -146,10 +189,14 @@
     return summed, jnp.where(iota((q, LANES), 1) < HEADS, top, totals)
 
 
+def copied(x, shape):
+    return jnp.broadcast_to(x[None], shape).astype(jnp.float32)
+
+
 def merge_kernel(parts_ref, out_ref):
     summed, side = merge(parts_ref[...])
-    out_ref[:, :, :C] = jnp.broadcast_to(summed[None], (out_ref.shape[0], *summed.shape))
-    out_ref[:, :, C:] = jnp.broadcast_to(side[None], (out_ref.shape[0], *side.shape))
+    out_ref[:, :, :C] = copied(summed, (out_ref.shape[0], *summed.shape))
+    out_ref[:, :, C:] = copied(side, (out_ref.shape[0], *side.shape))
 
 
 def attend_kernel(parts_ref, out_ref):
@@ -157,11 +204,12 @@
     q = side.shape[0]
     totals = pltpu.roll(side, LANES - HEADS, 1)
     totals = jnp.where(iota((q, LANES), 1) < HEADS, totals, 0.0)
-    out_ref[...] = summed / dot_exact(totals, widening())
+    attention = summed / dot_exact(totals, widening())
+    out_ref[...] = copied(attention, out_ref.shape).astype(out_ref.dtype)
 
 
 def finish_kernel(attention_ref, out_weight_ref, queries_ref, gain_ref, attended_ref, updated_ref):
-    attention = attention_ref[...].reshape(-1, C)[:PADDED].astype(jnp.bfloat16)
+    attention = attention_ref[...].astype(jnp.float32).reshape(-1, C)[:PADDED].astype(jnp.bfloat16)
     attended = dot(attention, out_weight_ref[...])[:QUERIES]
     attended_ref[...] = attended
     residual_sum = queries_ref[...] + attended
@@ -199,17 +247,17 @@
         [jnp.concatenate([part[:, :1], part[:, -1:]], axis=1) for part in (top, features, bottom)], axis=0
     )
     left, right = neighbours(edges, "cols", 1)
+    row_peers, col_peers = lax.axis_size("rows"), lax.axis_size("cols")
+    share = pl.cdiv(QUERIES, row_peers)
     pixels, part = local(
-        features, top, bottom, left, right, conv_weight, query_weight, kv_weight, queries, active_blocks
-    )
-    peers = lax.axis_size("cols")
-    share = 8
-    part = jnp.pad(part, ((0, peers * share - PADDED), (0, 0))).reshape(peers, share, PAYLOAD)
-    parts = lax.all_to_all(part, "cols", 0, 0)
-    copies = jax.ShapeDtypeStruct((lax.axis_size("rows"), share, PAYLOAD), jnp.float32)
-    parts = lax.all_to_all(on_device(merge_kernel, copies, parts), "rows", 0, 0)
-    attention = on_device(attend_kernel, jax.ShapeDtypeStruct((share, C), jnp.float32), parts)
-    attention = lax.all_gather(attention, "cols")
+        features, top, bottom, left, right, conv_weight, query_weight, kv_weight, queries, active_blocks,
+        (row_peers, share, PAYLOAD),
+    )
+    parts = lax.all_to_all(part, "rows", 0, 0)
+    copies = jax.ShapeDtypeStruct((col_peers, share, PAYLOAD), jnp.float32)
+    parts = lax.all_to_all(on_device(merge_kernel, copies, parts), "cols", 0, 0)
+    copies = jax.ShapeDtypeStruct((row_peers, share, C), jnp.bfloat16)
+    attention = lax.all_to_all(on_device(attend_kernel, copies, parts), "rows", 0, 0)
     out = jax.ShapeDtypeStruct((QUERIES, C), jnp.float32)
     attended, updated = on_device(
         finish_kernel, (out, out), attention, out_weight, queries, norm_gain.reshape(1, C)

time: 92.8 us -> 83.8 us (0.903)
  blocking collectives: 60.3 us -> 52.5 us
  local copies, waits for them, and re-layouts: 7.76 us -> 2.29 us
  Pallas kernels: 6.09 us -> 9.66 us
    all_gather x1 -> x0, blocking collectives: 16.3 us -> none  [body(): attention = lax.all_gather(attention, 'cols')]
    all_to_all x2 -> x3, blocking collectives: 44 us -> 52.5 us  [the longest x1 21.8 us: body(): parts = lax.all_to_all(part, 'rows', 0, 0)]
    unnamed x15 -> x14, local copies, waits for them, and re-layouts: 6.07 us -> 0.62 us
    pallas_call x1, Pallas kernels: 4.4 us -> 7.99 us  [local(): pl.pallas_call(local_kernel, out_shape=(pixels, jax.ShapeDtypeStruct(part...]
  transfers between devices with their start and end apart: 4 -> 4, of which waited for: 1 -> 1; matrix products, arithmetic and copies ran while one was open for 2% -> 1% of each run, Pallas kernels for 0% -> 0%
where the time goes in v1:
time: 83.8 us; the launch traced here: 83.3 us
  blocking collectives  52.5 us (63%)
  starting transfers between devices  16.9 us (20%)
  Pallas kernels  9.66 us (12%)
  local copies, waits for them, and re-layouts  2.29 us (3%)
  waiting for transfers between devices  1.14 us (1%)
    all_to_all x1, blocking collectives, body(): parts = lax.all_to_all(part, 'rows', 0, 0)  21.8 us
    all_to_all x1, blocking collectives, body(): parts = lax.all_to_all(on_device(merge_kernel, copies, parts), 'cols', 0, 0)  18.1 us
    ppermute x4, starting transfers between devices, neighbours(): return (lax.ppermute(last, axis, up), lax.ppermute(first, axis, down))  16.9 us
    all_to_all x1, blocking collectives, body(): lax.all_to_all(on_device(attend_kernel, copies, parts), 'rows', 0, 0)  12.6 us
    pallas_call x1, Pallas kernels, local(): pl.pallas_call(local_kernel, out_shape=(pixels, jax.ShapeDtypeStruct(part...  7.99 us
  transfers between devices with their start and end apart: 4, of which 1 were waited for; matrix products, arithmetic and copies ran while one was open for 1% of the time, Pallas kernels for 0%

profile of v1, /device:TPU:1, one launch (start us, length us, event | category | flops | bytes accessed | tf_op | source)
XLA Modules:
  0.0 83.3 jit_solution(13118946196649536922)
XLA Ops:
  0.6 0.7 fusion.1
  1.4 1.3 %collective-permute-start.1 = (bf16[1,16,256]{2,1,0:T(8,128)(2,1)S(1)}, bf16[1,16,256]{2,1,0:T(8,128)(2,1)S(1)}, u32[]{:S(2)}, u32[]{:S(2)}) collective-permute-start(bf16[1,16,256]{2,1,0:T(8,128)(2,1)S(1)} %get-tuple-element.13), channel_id=1, source_target_pairs={{16,0},{32,16},{48,32},{64,48},{80,64},{96,80},{112,96},{128,112},... | collective-permute-start | bytes 24584 | tf_op jit(solution)/shard_map/ppermute | solution.py:239
  2.6 5.5 %collective-permute-start = (bf16[1,16,256]{2,1,0:T(8,128)(2,1)S(1)}, bf16[1,16,256]{2,1,0:T(8,128)(2,1)S(1)}, u32[]{:S(2)}, u32[]{:S(2)}) collective-permute-start(bf16[1,16,256]{2,1,0:T(8,128)(2,1)S(1)} %get-tuple-element.14), channel_id=1, source_target_pairs={{0,16},{16,32},{32,48},{48,64},{64,80},{80,96},{96,112},{112,128},... | collective-permute-start | bytes 24584 | tf_op jit(solution)/shard_map/ppermute | solution.py:239
  8.1 0.9 %fusion = (bf16[16,1,256]{2,1,0:T(2,128)(2,1)S(1)}, bf16[16,1,256]{2,1,0:T(2,128)(2,1)S(1)}) fusion(bf16[16,16,256]{2,1,0:T(8,128)(2,1)} %x_hbm.1), kind=kLoop, calls=%fused_computation.1 | loop fusion | bytes 32768 | tf_op jit(solution)/shard_map/slice | solution.py:247
  9.0 0.0 collective-permute-done.1.bottom_ref
  9.0 0.0 copy-start.3
  9.0 0.0 collective-permute-done.top_ref
  9.1 0.0 copy-start.4
  9.2 8.3 %collective-permute-start.3 = (bf16[18,1,256]{2,1,0:T(2,128)(2,1)S(1)}, bf16[18,1,256]{2,1,0:T(2,128)(2,1)S(1)}, u32[]{:S(2)}, u32[]{:S(2)}) collective-permute-start(bf16[18,1,256]{2,1,0:T(2,128)(2,1)S(1)} %get-tuple-element.15), channel_id=1, source_target_pairs={{1,0},{2,1},{3,2},{4,3},{5,4},{6,5},{7,6},{8,7},{9,8},{10,9},{11,1... | collective-permute-start | bytes 27656 | tf_op jit(solution)/shard_map/ppermute | solution.py:239
  17.4 1.9 %collective-permute-start.2 = (bf16[18,1,256]{2,1,0:T(2,128)(2,1)S(1)}, bf16[18,1,256]{2,1,0:T(2,128)(2,1)S(1)}, u32[]{:S(2)}, u32[]{:S(2)}) collective-permute-start(bf16[18,1,256]{2,1,0:T(2,128)(2,1)S(1)} %get-tuple-element.16), channel_id=1, source_target_pairs={{0,1},{1,2},{2,3},{3,4},{4,5},{5,6},{6,7},{7,8},{8,9},{9,10},{10,1... | collective-permute-start | bytes 27656 | tf_op jit(solution)/shard_map/ppermute | solution.py:239
  19.4 0.0 collective-permute-done.3.right_ref
  19.4 0.0 copy-start.5
  19.4 1.1 %collective-permute-done.2.left_ref = bf16[18,1,256]{2,1,0:T(2,128)(2,1)S(1)} collective-permute-done((bf16[18,1,256]{2,1,0:T(2,128)(2,1)S(1)}, bf16[18,1,256]{2,1,0:T(2,128)(2,1)S(1)}, u32[]{:S(2)}, u32[]{:S(2)}) %collective-permute-start.2) | collective-permute-done | bytes 9248 | tf_op jit(solution)/shard_map/ppermute | solution.py:239
  20.5 0.0 copy-start.6
  20.5 0.0 copy-done.3
  20.5 0.0 copy-done.4
  20.5 0.0 copy-done.5
  20.5 0.6 copy-done.6
  21.1 0.0 copy-start
  21.1 0.0 copy-start.1
  21.1 0.0 copy-start.2
  21.1 8.0 %shard_map.103 = (bf16[32,32,256]{2,1,0:T(8,128)(2,1)}, f32[32,4,384]{2,1,0:T(4,128)}) custom-call(bf16[16,16,256]{2,1,0:T(8,128)(2,1)} %x_hbm.1, bf16[1,16,256]{2,1,0:T(8,128)(2,1)} %copy-done.4, bf16[1,16,256]{2,1,0:T(8,128)(2,1)} %copy-done.3, bf16[18,1,256]{2,1,0:T(2,128)(2,1)} %copy-done.6, bf16[18,1,256]{2,1,0:T(2,128)(2,1)} %copy-done.5, ...), custom_call_target="tpu_custom_call" | custom-call | flops 2000000000 | bytes 4000000 | tf_op jit(solution)/shard_map/pallas_call | solution.py:153
  29.1 21.8 %all_to_all.15.parts_ref = f32[32,4,384]{2,1,0:T(4,128)S(1)} all-to-all(f32[32,4,384]{2,1,0:T(4,128)} %get-tuple-element.8), channel_id=1, replica_groups=mesh['rows'=32,'cols'=16] {'rows'}, dimensions={0} | all-to-all | bytes 393216 | tf_op jit(solution)/shard_map/all_to_all | solution.py:256
  51.0 0.3 shard_map.104
  51.3 18.1 %all_to_all.16.parts_ref = f32[16,4,384]{2,1,0:T(4,128)S(1)} all-to-all(f32[16,4,384]{2,1,0:T(4,128)S(1)} %shard_map.104), channel_id=1, replica_groups=mesh['rows'=32,'cols'=16] {'cols'}, dimensions={0} | all-to-all | bytes 196608 | tf_op jit(solution)/shard_map/all_to_all | solution.py:258
  69.4 0.4 shard_map.105
  69.8 12.6 %all_to_all.17.attention_ref = bf16[32,4,256]{2,1,0:T(4,128)(2,1)S(1)} all-to-all(bf16[32,4,256]{2,1,0:T(4,128)(2,1)S(1)} %shard_map.105), channel_id=1, replica_groups=mesh['rows'=32,'cols'=16] {'rows'}, dimensions={0} | all-to-all | bytes 131072 | tf_op jit(solution)/shard_map/all_to_all | solution.py:260
  82.3 0.0 copy-done
  82.3 0.0 copy-done.1
  82.3 0.0 copy-done.2
  82.4 1.0 %shard_map.106 = (f32[100,256]{1,0:T(8,128)}, f32[100,256]{1,0:T(8,128)}) custom-call(bf16[32,4,256]{2,1,0:T(4,128)(2,1)S(1)} %all_to_all.17.attention_ref, bf16[256,256]{1,0:T(8,128)(2,1)S(1)} %copy-done, f32[100,256]{1,0:T(8,128)S(1)} %copy-done.1, f32[1,256]{1,0:T(1,128)S(1)} %bitcast.2), custom_call_target="tpu_custom_call" | custom-call | flops 10000000 | bytes 500000 | tf_op jit(solution)/shard_map/pallas_call | solution.py:223
  (4 shorter events, 0.1 us)
Async XLA Ops:
  1.4 7.7 %collective-permute-start.1 = (bf16[1,16,256]{2,1,0:T(8,128)(2,1)S(1)}, bf16[1,16,256]{2,1,0:T(8,128)(2,1)S(1)}, u32[]{:S(2)}, u32[]{:S(2)}) collective-permute-start(bf16[1,16,256]{2,1,0:T(8,128)(2,1)S(1)} %get-tuple-element.13), channel_id=1, source_target_pairs={{16,0},{32,16},{48,32},{64,48},{80,64},{96,80},{112,96},{128,112},... | collective-permute-start | bytes 24584 | tf_op jit(solution)/shard_map/ppermute | solution.py:239
  2.6 6.4 %collective-permute-start = (bf16[1,16,256]{2,1,0:T(8,128)(2,1)S(1)}, bf16[1,16,256]{2,1,0:T(8,128)(2,1)S(1)}, u32[]{:S(2)}, u32[]{:S(2)}) collective-permute-start(bf16[1,16,256]{2,1,0:T(8,128)(2,1)S(1)} %get-tuple-element.14), channel_id=1, source_target_pairs={{0,16},{16,32},{32,48},{48,64},{64,80},{80,96},{96,112},{112,128},... | collective-permute-start | bytes 24584 | tf_op jit(solution)/shard_map/ppermute | solution.py:239
  9.0 11.5 %copy-start.3 = (bf16[1,16,256]{2,1,0:T(8,128)(2,1)}, bf16[1,16,256]{2,1,0:T(8,128)(2,1)S(1)}, u32[]{:S(2)}) copy-start(bf16[1,16,256]{2,1,0:T(8,128)(2,1)S(1)} %collective-permute-done.1.bottom_ref) | copy-start | bytes 24580
  9.1 11.5 %copy-start.4 = (bf16[1,16,256]{2,1,0:T(8,128)(2,1)}, bf16[1,16,256]{2,1,0:T(8,128)(2,1)S(1)}, u32[]{:S(2)}) copy-start(bf16[1,16,256]{2,1,0:T(8,128)(2,1)S(1)} %collective-permute-done.top_ref) | copy-start | bytes 24580
  9.2 10.2 %collective-permute-start.3 = (bf16[18,1,256]{2,1,0:T(2,128)(2,1)S(1)}, bf16[18,1,256]{2,1,0:T(2,128)(2,1)S(1)}, u32[]{:S(2)}, u32[]{:S(2)}) collective-permute-start(bf16[18,1,256]{2,1,0:T(2,128)(2,1)S(1)} %get-tuple-element.15), channel_id=1, source_target_pairs={{1,0},{2,1},{3,2},{4,3},{5,4},{6,5},{7,6},{8,7},{9,8},{10,9},{11,1... | collective-permute-start | bytes 27656 | tf_op jit(solution)/shard_map/ppermute | solution.py:239
  17.4 3.1 %collective-permute-start.2 = (bf16[18,1,256]{2,1,0:T(2,128)(2,1)S(1)}, bf16[18,1,256]{2,1,0:T(2,128)(2,1)S(1)}, u32[]{:S(2)}, u32[]{:S(2)}) collective-permute-start(bf16[18,1,256]{2,1,0:T(2,128)(2,1)S(1)} %get-tuple-element.16), channel_id=1, source_target_pairs={{0,1},{1,2},{2,3},{3,4},{4,5},{5,6},{6,7},{7,8},{8,9},{9,10},{10,1... | collective-permute-start | bytes 27656 | tf_op jit(solution)/shard_map/ppermute | solution.py:239
  19.4 1.2 %copy-start.5 = (bf16[18,1,256]{2,1,0:T(2,128)(2,1)}, bf16[18,1,256]{2,1,0:T(2,128)(2,1)S(1)}, u32[]{:S(2)}) copy-start(bf16[18,1,256]{2,1,0:T(2,128)(2,1)S(1)} %collective-permute-done.3.right_ref) | copy-start | bytes 27652
  20.5 0.6 copy-start.6
  21.1 61.2 %copy-start = (bf16[256,256]{1,0:T(8,128)(2,1)S(1)}, bf16[256,256]{1,0:T(8,128)(2,1)}, u32[]{:S(2)}) copy-start(bf16[256,256]{1,0:T(8,128)(2,1)} %out_weight_ref.1) | copy-start | bytes 393220
  21.1 61.2 %copy-start.1 = (f32[100,256]{1,0:T(8,128)S(1)}, f32[100,256]{1,0:T(8,128)}, u32[]{:S(2)}) copy-start(f32[100,256]{1,0:T(8,128)} %queries_ref.1) | copy-start | bytes 307204
  21.1 61.2 %copy-start.2 = (f32[256]{0:T(256)S(1)}, f32[256]{0:T(256)}, u32[]{:S(2)}) copy-start(f32[256]{0:T(256)} %param.14) | copy-start | bytes 3076

commit v2 on v1

v2 whole, which is shorter than its diff:
```python
import functools

import jax
import jax.numpy as jnp
from jax import lax
from jax.experimental import pallas as pl
from jax.experimental.pallas import tpu as pltpu
from jax.sharding import PartitionSpec as P

QUERIES = 100
PADDED = 104
HEADS = 8
HEAD = 32
BLOCK = 32
C = 256
LANES = 128
ROWS_IN = 16
COLS_IN = 16
LIST = 32
HALF = HEADS // 2
SHARE = 7
TILE = 8
HALVES = 2 * PADDED

masked_low = -1e30
tap_table = (((1, 1), (0, 3)), ((1, 2), (2, 0)))
query_chunks = ((0, 40), (40, 32), (72, 32))


def dot(a, b):
    return jnp.dot(a, b, preferred_element_type=jnp.float32)


def dot_exact(a, b):
    return jnp.dot(a, b, preferred_element_type=jnp.float32, precision=lax.Precision.HIGHEST)


def iota(shape, dim):
    return lax.broadcasted_iota(jnp.int32, shape, dim)


def local_kernel(
    x_hbm, top_hbm, bottom_hbm, left_hbm, right_hbm, weight_hbm, query_weight_hbm, kv_weight_hbm,
    queries_hbm, named_hbm, pixels_hbm, part_hbm,
    padded, left_ref, right_ref, weight_ref, query_weight_ref, kv_weight_ref, queries_ref, named_ref, pixels_ref, part_ref,
    shifted, joined, wide_queries, keys, values, flags, spread, half_sums, half_side, arrived, sent
):
    def fetch(source, target, slot):
        copy = pltpu.make_async_copy(source, target, arrived.at[slot])
        copy.start()
        return copy

    fetch_queries = fetch(queries_hbm, queries_ref, 0)
    fetch_query_weight = fetch(query_weight_hbm, query_weight_ref, 1)
    fetch_named = fetch(named_hbm, named_ref, 2)
    fetch_features = [
        fetch(top_hbm, padded.at[pl.ds(0, 1)], 3),
        fetch(x_hbm, padded.at[pl.ds(1, ROWS_IN)], 9),
        fetch(bottom_hbm, padded.at[pl.ds(ROWS_IN + 1, 1)], 10),
        fetch(left_hbm, left_ref, 11),
        fetch(right_hbm, right_ref, 12),
    ]
    fetch_weight = {}
    for a in range(2):
        for _, row_kernel in tap_table[a]:
            fetch_weight[row_kernel] = fetch(
                weight_hbm.at[row_kernel], weight_ref.at[row_kernel], 4 + row_kernel
            )
        if a == 0:
            fetch_kv_weight = fetch(kv_weight_hbm, kv_weight_ref, 8)

    own_head = iota((1, HEADS, C), 2) // HEAD == iota((1, HEADS, C), 1)
    fetch_queries.wait()
    fetch_query_weight.wait()
    projected = dot(queries_ref[...].astype(jnp.bfloat16), query_weight_ref[...]) * HEAD ** (-0.5)
    spread[:QUERIES] = projected
    spread[QUERIES:] = jnp.zeros((PADDED - QUERIES, C), jnp.float32)
    each = jnp.where(own_head, spread[...][:, None, :], 0.0)
    wide_queries[...] = each.reshape(PADDED * HEADS, C).astype(jnp.bfloat16)

    fetch_named.wait()
    block_id = lax.axis_index("rows") * lax.axis_size("cols") + lax.axis_index("cols")
    hits = (named_ref[...] == block_id).astype(jnp.bfloat16)
    flags[:QUERIES] = lax.dot_general(
        hits, jnp.ones((hits.shape[0], LANES), jnp.bfloat16), (((0,), (0,)), ((), ())), preferred_element_type=jnp.float32
    )
    flags[QUERIES:] = jnp.zeros((PADDED - QUERIES, LANES), jnp.float32)

    for copy in fetch_features:
        copy.wait()
    height = ROWS_IN + 2
    middle = padded[...]
    shifted[1] = middle.reshape(height * COLS_IN, C)
    middle = middle.astype(jnp.float32)
    column = iota((height, COLS_IN, C), 1)
    left = left_ref[...].astype(jnp.float32)
    right = right_ref[...].astype(jnp.float32)
    before = jnp.where(column == 0, left, pltpu.roll(middle, 1, 1))
    after = jnp.where(column == COLS_IN - 1, right, pltpu.roll(middle, COLS_IN - 1, 1))
    shifted[0] = before.astype(jnp.bfloat16).reshape(height * COLS_IN, C)
    shifted[2] = after.astype(jnp.bfloat16).reshape(height * COLS_IN, C)

    area = ROWS_IN * COLS_IN
    for a in range(2):
        for _, row_kernel in tap_table[a]:
            fetch_weight[row_kernel].wait()
        if a == 0:
            fetch_kv_weight.wait()
        for b in range(2):
            total = None
            for row_offset, row_kernel in tap_table[a]:
                for col_offset, col_kernel in tap_table[b]:
                    window = shifted[col_offset, row_offset * COLS_IN : row_offset * COLS_IN + area]
                    term = dot(window, weight_ref[row_kernel, col_kernel])
                    total = term if total is None else total + term
            for half in range(2):
                part = total[:, half * LANES : (half + 1) * LANES].reshape(ROWS_IN, COLS_IN, LANES)
                joined[half, :, a, pl.ds(b, COLS_IN, stride=2), :] = part
            key_value = dot(total.astype(jnp.bfloat16), kv_weight_ref[...]).astype(jnp.bfloat16)
            at = (2 * a + b) * area
            keys[at : at + area] = key_value[:, :C]
            values[at : at + area] = key_value[:, C:]
    for half in range(2):
        part = joined[half].reshape(2 * ROWS_IN, 2 * COLS_IN, LANES).astype(jnp.bfloat16)
        pixels_ref[:, :, half * LANES : (half + 1) * LANES] = part
    send_pixels = pltpu.make_async_copy(pixels_ref, pixels_hbm, sent.at[0])
    send_pixels.start()

    ones = jnp.ones((4 * area, LANES), jnp.bfloat16)
    for start, count in query_chunks:
        rows = slice(start * HEADS, (start + count) * HEADS)
        now = lax.dot_general(
            wide_queries[rows], keys[...], (((1,), (1,)), ((), ())), preferred_element_type=jnp.float32
        )
        highest = jnp.max(now, axis=1, keepdims=True)
        weights = jnp.exp(now - highest).astype(jnp.bfloat16)
        summed = dot(weights, values[...]).reshape(count, HEADS, C)
        totals = dot(weights, ones).reshape(count, HEADS, LANES)
        highest = jnp.broadcast_to(highest, (count * HEADS, LANES)).reshape(count, HEADS, LANES)
        here = flags[start : start + count] > 0.0
        summed = jnp.sum(jnp.where(own_head, summed, 0.0), axis=1)
        lane = iota((count, HEADS, LANES), 2)
        head = iota((count, HEADS, LANES), 1)
        for half in range(2):
            at = half * PADDED + start
            into = slice(at, at + count)
            half_sums[into] = jnp.where(here, summed[:, half * LANES : (half + 1) * LANES], 0.0)
            row = lax.rem(iota((count, HEADS, LANES), 0) + at, SHARE)
            slot = lane - TILE * row
            own = head - HALF * half
            own = jnp.where((own >= 0) & (own < HALF), own, -TILE * LANES)
            is_highest = slot == own
            placed = jnp.where(is_highest, highest, 0.0) + jnp.where(slot == own + HALF, totals, 0.0)
            absent = jnp.sum(jnp.where(is_highest, masked_low, 0.0), axis=1)
            half_side[into] = jnp.where(here, jnp.sum(placed, axis=1), absent)

    for buffer in (half_sums, half_side):
        buffer[HALVES:] = jnp.zeros((buffer.shape[0] - HALVES, LANES), jnp.float32)
    filled = pl.cdiv(HALVES, SHARE)
    for index in range(filled):
        rows = slice(index * SHARE, (index + 1) * SHARE)
        part_ref[index, :SHARE] = half_sums[rows]
        part_ref[index, SHARE:] = jnp.sum(half_side[rows], axis=0, keepdims=True)
    if filled < part_ref.shape[0]:
        part_ref[filled:] = jnp.zeros((part_ref.shape[0] - filled, TILE, LANES), jnp.float32)
    send_part = pltpu.make_async_copy(part_ref, part_hbm, sent.at[1])
    send_part.start()
    send_pixels.wait()
    send_part.wait()


def local(x, top, bottom, left, right, weight, query_weight, kv_weight, queries, active_blocks, shares):
    area = ROWS_IN * COLS_IN
    pixels = jax.ShapeDtypeStruct((2 * ROWS_IN, 2 * COLS_IN, C), jnp.bfloat16)
    padded = jax.ShapeDtypeStruct((ROWS_IN + 2, COLS_IN, C), jnp.bfloat16)
    part = jax.ShapeDtypeStruct((shares, TILE, LANES), jnp.float32)
    anywhere = pl.BlockSpec(memory_space=pl.ANY)
    named = active_blocks.T
    return pl.pallas_call(
        local_kernel,
        out_shape=(pixels, part),
        in_specs=[anywhere] * 10,
        out_specs=[anywhere] * 2,
        scratch_shapes=[pltpu.VMEM(t.shape, t.dtype) for t in (padded, left, right, weight, query_weight, kv_weight, queries, named, pixels, part)]
        + [
            pltpu.VMEM((3, (ROWS_IN + 2) * COLS_IN, C), jnp.bfloat16),
            pltpu.VMEM((2, ROWS_IN, 2, 2 * COLS_IN, LANES), jnp.float32),
            pltpu.VMEM((PADDED * HEADS, C), jnp.bfloat16),
            pltpu.VMEM((4 * area, C), jnp.bfloat16),
            pltpu.VMEM((4 * area, C), jnp.bfloat16),
            pltpu.VMEM((PADDED, LANES), jnp.float32),
            pltpu.VMEM((PADDED, C), jnp.float32),
            pltpu.VMEM((HALVES + TILE, LANES), jnp.float32),
            pltpu.VMEM((HALVES + TILE, LANES), jnp.float32),
            pltpu.SemaphoreType.DMA((13,)),
            pltpu.SemaphoreType.DMA((2,)),
        ],
        compiler_params=pltpu.CompilerParams(vmem_limit_bytes=60 << 20),
        cost_estimate=pl.CostEstimate(flops=2_000_000_000, bytes_accessed=4_000_000, transcendentals=800_000),
    )(x, top, bottom, left, right, weight, query_weight, kv_weight, queries, named)


def widened(side, first):
    n = side.shape[0]
    lane = iota((n, TILE, LANES), 2)
    own = lane // TILE == iota((n, TILE, LANES), 1)
    rows = jnp.where(own, jnp.broadcast_to(side, (n, TILE, LANES)), 0.0).reshape(n * TILE, LANES)
    spread = iota((LANES, LANES), 0) % TILE - first == iota((LANES, LANES), 1) // HEAD
    return dot_exact(rows, spread.astype(jnp.float32)).reshape(n, TILE, LANES)


def merge(parts):
    n = parts.shape[0]
    side = parts[:, SHARE:, :]
    lane = iota((n, 1, LANES), 2)
    is_highest = (lane % TILE < HALF) & (lane < SHARE * TILE)
    top = jnp.max(side, axis=0, keepdims=True)
    factor = jnp.where(is_highest, jnp.exp(jnp.where(is_highest, side - top, 0.0)), 0.0)
    summed = jnp.sum(parts * widened(factor, 0), axis=0)
    moved = pltpu.roll(factor.reshape(n, LANES), HALF, 1)
    totals = jnp.sum(side.reshape(n, LANES) * moved, axis=0, keepdims=True)
    return summed, jnp.where(is_highest[0], top[0], totals)


def merge_kernel(parts_ref, out_ref):
    summed, side = merge(parts_ref[...])
    row = iota((TILE, LANES), 0)
    merged = jnp.where(row == SHARE, jnp.broadcast_to(side, (TILE, LANES)), summed)
    out_ref[...] = jnp.broadcast_to(merged[None], out_ref.shape)


def attend_kernel(parts_ref, out_ref):
    summed, side = merge(parts_ref[...])
    totals = widened(side[None], HALF)[0]
    attention = jnp.where(iota((TILE, LANES), 0) == SHARE, 0.0, summed / totals)
    out_ref[...] = jnp.broadcast_to(attention[None], out_ref.shape).astype(out_ref.dtype)


def finish_kernel(attention_ref, out_weight_ref, queries_ref, gain_ref, attended_ref, updated_ref, halves):
    shares = attention_ref[...].astype(jnp.float32)
    for index in range(pl.cdiv(HALVES, SHARE)):
        halves[index * SHARE : (index + 1) * SHARE] = shares[index, :SHARE]
    attended = jnp.zeros((PADDED, C), jnp.float32)
    for half in range(2):
        attention = halves[half * PADDED : (half + 1) * PADDED].astype(jnp.bfloat16)
        attended += dot(attention, out_weight_ref[half * LANES : (half + 1) * LANES])
    attended = attended[:QUERIES]
    attended_ref[...] = attended
    residual_sum = queries_ref[...] + attended
    average = jnp.mean(residual_sum, axis=1, keepdims=True)
    centred = residual_sum - average
    deviation = jnp.mean(centred * centred, axis=1, keepdims=True)
    updated_ref[...] = centred * lax.rsqrt(deviation + 1e-05) * gain_ref[...]


def on_device(kernel, out_shape, *operands, scratch=()):
    return pl.pallas_call(
        kernel,
        out_shape=out_shape,
        in_specs=[pl.BlockSpec(memory_space=pltpu.VMEM)] * len(operands),
        out_specs=jax.tree.map(lambda _: pl.BlockSpec(memory_space=pltpu.VMEM), out_shape),
        scratch_shapes=scratch,
        compiler_params=pltpu.CompilerParams(vmem_limit_bytes=32 << 20),
        cost_estimate=pl.CostEstimate(flops=10_000_000, bytes_accessed=500_000, transcendentals=10_000),
    )(*operands)


def neighbours(x, axis, dim):
    peers = lax.axis_size(axis)
    last = lax.slice_in_dim(x, x.shape[dim] - 1, x.shape[dim], axis=dim)
    first = lax.slice_in_dim(x, 0, 1, axis=dim)
    odd = lax.axis_index(axis) % 2 == 1
    swaps = []
    for start, edge in ((0, jnp.where(odd, first, last)), (1, jnp.where(odd, last, first))):
        pairs = [(i, i + 1) for i in range(start, peers - 1, 2)]
        swaps.append(lax.ppermute(edge, axis, pairs + [(j, i) for i, j in pairs]))
    return jnp.where(odd, swaps[0], swaps[1]), jnp.where(odd, swaps[1], swaps[0])


def body(
    features, conv_weight, query_weight, kv_weight, out_weight, queries, norm_gain, active_blocks
):
    top, bottom = neighbours(features, "rows", 0)
    edges = jnp.concatenate(
        [jnp.concatenate([part[:, :1], part[:, -1:]], axis=1) for part in (top, features, bottom)], axis=0
    )
    left, right = neighbours(edges, "cols", 1)
    row_peers, col_peers = lax.axis_size("rows"), lax.axis_size("cols")
    pixels, part = local(
        features, top, bottom, left, right, conv_weight, query_weight, kv_weight, queries, active_blocks, row_peers
    )
    parts = lax.all_to_all(part, "rows", 0, 0)
    copies = jax.ShapeDtypeStruct((col_peers, TILE, LANES), jnp.float32)
    parts = lax.all_to_all(on_device(merge_kernel, copies, parts), "cols", 0, 0)
    copies = jax.ShapeDtypeStruct((row_peers, TILE, LANES), jnp.bfloat16)
    attention = lax.all_to_all(on_device(attend_kernel, copies, parts), "rows", 0, 0)
    out = jax.ShapeDtypeStruct((QUERIES, C), jnp.float32)
    attended, updated = on_device(
        finish_kernel, (out, out), attention, out_weight, queries, norm_gain.reshape(1, C),
        scratch=[pltpu.VMEM((HALVES + TILE, LANES), jnp.float32)],
    )
    return (pixels, attended, updated)


def solution(mesh):
    placed = (P("rows", "cols", None), P(), P(), P(), P(), P(), P(), P())
    return jax.shard_map(
        body,
        mesh=mesh,
        in_specs=placed,
        out_specs=(P("rows", "cols", None), P(), P()),
        check_vma=False,
    )
```

time: 83.8 us -> 78.3 us (0.934)
  blocking collectives: 52.5 us -> 49.2 us
  other arithmetic: 0.05 us -> 1.49 us
  local copies, waits for them, and re-layouts: 2.29 us -> 0.93 us
  starting transfers between devices: 16.9 us -> 15.7 us
  Pallas kernels: 9.66 us -> 8.55 us
    all_to_all x1, blocking collectives: 18.1 us -> 16.3 us  [body(): parts = lax.all_to_all(on_device(merge_kernel, copies, parts), 'cols', 0, 0)]
    select_n x0 -> x4, other arithmetic: none -> 1.44 us  [the longest x2 0.78 us: neighbours(): jnp.where(odd, last, first)]
    ppermute x4, starting transfers between devices: 16.9 us -> 15.7 us  [neighbours(): swaps.append(lax.ppermute(edge, axis, pairs + [(j, i) for i, j in pairs]))]
    all_to_all x1, blocking collectives: 21.8 us -> 20.8 us  [body(): parts = lax.all_to_all(part, 'rows', 0, 0)]
    pallas_call x1, Pallas kernels: 7.99 us -> 6.93 us  [local(): pl.pallas_call(local_kernel, out_shape=(pixels, part), in_specs=[anywhere...]
  transfers between devices with their start and end apart: 4 -> 4, of which waited for: 1 -> 2; matrix products, arithmetic and copies ran while one was open for 1% -> 1% of each run, Pallas kernels for 0% -> 0%
where the time goes in v2:
time: 78.3 us; the launch traced here: 77.8 us
  blocking collectives  49.2 us (63%)
  starting transfers between devices  15.7 us (20%)
  Pallas kernels  8.55 us (11%)
  other arithmetic  1.49 us (2%)
  waiting for transfers between devices  1.24 us (2%)
  local copies, waits for them, and re-layouts  0.93 us (1%)
    all_to_all x1, blocking collectives, body(): parts = lax.all_to_all(part, 'rows', 0, 0)  20.8 us
    all_to_all x1, blocking collectives, body(): parts = lax.all_to_all(on_device(merge_kernel, copies, parts), 'cols', 0, 0)  16.3 us
    ppermute x4, starting transfers between devices, neighbours(): swaps.append(lax.ppermute(edge, axis, pairs + [(j, i) for i, j in pairs]))  15.7 us
    all_to_all x1, blocking collectives, body(): lax.all_to_all(on_device(attend_kernel, copies, parts), 'rows', 0, 0)  12.1 us
    pallas_call x1, Pallas kernels, local(): pl.pallas_call(local_kernel, out_shape=(pixels, part), in_specs=[anywhere...  6.93 us
    pallas_call x3, Pallas kernels, on_device(): pl.pallas_call(kernel, out_shape=out_shape, in_specs=[pl.BlockSpec(memory...  1.62 us
  transfers between devices with their start and end apart: 4, of which 2 were waited for; matrix products, arithmetic and copies ran while one was open for 1% of the time, Pallas kernels for 0%

profile of v2, /device:TPU:1, one launch (start us, length us, event | category | flops | bytes accessed | tf_op | source)
XLA Modules:
  0.0 77.8 jit_solution(6208629835197987875)
XLA Ops:
  0.6 0.7 broadcast_select_fusion.6
  1.4 0.6 collective-permute-start.1
  2.0 8.2 %collective-permute-start = (bf16[1,16,256]{2,1,0:T(8,128)(2,1)S(1)}, bf16[1,16,256]{2,1,0:T(8,128)(2,1)S(1)}, u32[]{:S(2)}, u32[]{:S(2)}) collective-permute-start(bf16[1,16,256]{2,1,0:T(8,128)(2,1)S(1)} %get-tuple-element.14), channel_id=1, source_target_pairs={{0,16},{32,48},{64,80},{96,112},{128,144},{160,176},{192,208},{224... | collective-permute-start | bytes 24584 | tf_op jit(solution)/shard_map/ppermute | solution.py:276
  10.2 0.9 %fusion = (bf16[16,1,256]{2,1,0:T(2,128)(2,1)S(1)}, bf16[16,1,256]{2,1,0:T(2,128)(2,1)S(1)}) fusion(bf16[16,16,256]{2,1,0:T(8,128)(2,1)} %x_hbm.1), kind=kLoop, calls=%fused_computation.9 | loop fusion | bytes 32768 | tf_op jit(solution)/shard_map/slice | solution.py:285
  11.1 0.0 collective-permute-done.1
  11.1 0.1 collective-permute-done
  11.2 0.0 copy-start.3
  11.2 0.0 copy-start.4
  11.4 4.9 %collective-permute-start.3 = (bf16[18,1,256]{2,1,0:T(2,128)(2,1)S(1)}, bf16[18,1,256]{2,1,0:T(2,128)(2,1)S(1)}, u32[]{:S(2)}, u32[]{:S(2)}) collective-permute-start(bf16[18,1,256]{2,1,0:T(2,128)(2,1)S(1)} %get-tuple-element.17), channel_id=1, source_target_pairs={{1,2},{3,4},{5,6},{7,8},{9,10},{11,12},{13,14},{2,1},{4,3},{6,5},{... | collective-permute-start | bytes 27656 | tf_op jit(solution)/shard_map/ppermute | solution.py:276
  16.3 1.9 %collective-permute-start.2 = (bf16[18,1,256]{2,1,0:T(2,128)(2,1)S(1)}, bf16[18,1,256]{2,1,0:T(2,128)(2,1)S(1)}, u32[]{:S(2)}, u32[]{:S(2)}) collective-permute-start(bf16[18,1,256]{2,1,0:T(2,128)(2,1)S(1)} %get-tuple-element.18), channel_id=1, source_target_pairs={{0,1},{2,3},{4,5},{6,7},{8,9},{10,11},{12,13},{14,15},{1,0},{3,2},... | collective-permute-start | bytes 27656 | tf_op jit(solution)/shard_map/ppermute | solution.py:276
  18.2 0.0 collective-permute-done.3
  18.2 1.1 %collective-permute-done.2 = bf16[18,1,256]{2,1,0:T(2,128)(2,1)S(1)} collective-permute-done((bf16[18,1,256]{2,1,0:T(2,128)(2,1)S(1)}, bf16[18,1,256]{2,1,0:T(2,128)(2,1)S(1)}, u32[]{:S(2)}, u32[]{:S(2)}) %collective-permute-start.2) | collective-permute-done | bytes 9248 | tf_op jit(solution)/shard_map/ppermute | solution.py:276
  19.4 0.7 broadcast_select_fusion
  20.0 0.0 copy-done.3
  20.0 0.0 copy-done.4
  20.0 0.0 copy-start
  20.0 0.0 copy-start.1
  20.1 0.0 copy-start.2
  20.1 6.9 %shard_map.103 = (bf16[32,32,256]{2,1,0:T(8,128)(2,1)}, f32[32,8,128]{2,1,0:T(8,128)}) custom-call(bf16[16,16,256]{2,1,0:T(8,128)(2,1)} %x_hbm.1, bf16[1,16,256]{2,1,0:T(8,128)(2,1)} %copy-done.4, bf16[1,16,256]{2,1,0:T(8,128)(2,1)} %copy-done.3, bf16[18,1,256]{2,1,0:T(2,128)(2,1)} %get-tuple-element.16.left_hbm, ...), custom_call_target="tpu_custom_call" | custom-call | flops 2000000000 | bytes 4000000 | tf_op jit(solution)/shard_map/pallas_call | solution.py:179
  27.0 20.8 %all_to_all.15.parts_ref = f32[32,8,128]{2,1,0:T(8,128)S(1)} all-to-all(f32[32,8,128]{2,1,0:T(8,128)} %get-tuple-element.8), channel_id=1, replica_groups=mesh['rows'=32,'cols'=16] {'rows'}, dimensions={0} | all-to-all | bytes 262144 | tf_op jit(solution)/shard_map/all_to_all | solution.py:292
  47.8 0.3 shard_map.104
  48.1 16.3 %all_to_all.16.parts_ref = f32[16,8,128]{2,1,0:T(8,128)S(1)} all-to-all(f32[16,8,128]{2,1,0:T(8,128)S(1)} %shard_map.104), channel_id=1, replica_groups=mesh['rows'=32,'cols'=16] {'cols'}, dimensions={0} | all-to-all | bytes 131072 | tf_op jit(solution)/shard_map/all_to_all | solution.py:294
  64.4 0.3 shard_map.105
  64.7 12.1 %all_to_all.17.attention_ref = bf16[32,8,128]{2,1,0:T(8,128)(2,1)S(1)} all-to-all(bf16[32,8,128]{2,1,0:T(8,128)(2,1)S(1)} %shard_map.105), channel_id=1, replica_groups=mesh['rows'=32,'cols'=16] {'rows'}, dimensions={0} | all-to-all | bytes 131072 | tf_op jit(solution)/shard_map/all_to_all | solution.py:296
  76.8 0.0 copy-done
  76.8 0.0 copy-done.1
  76.8 0.0 copy-done.2
  76.8 1.0 %shard_map.106 = (f32[100,256]{1,0:T(8,128)}, f32[100,256]{1,0:T(8,128)}) custom-call(bf16[32,8,128]{2,1,0:T(8,128)(2,1)S(1)} %all_to_all.17.attention_ref, bf16[256,256]{1,0:T(8,128)(2,1)S(1)} %copy-done, f32[100,256]{1,0:T(8,128)S(1)} %copy-done.1, f32[1,256]{1,0:T(1,128)S(1)} %bitcast.2), custom_call_target="tpu_custom_call" | custom-call | flops 10000000 | bytes 500000 | tf_op jit(solution)/shard_map/pallas_call | solution.py:257
  (4 shorter events, 0.1 us)
Async XLA Ops:
  1.4 9.8 %collective-permute-start.1 = (bf16[1,16,256]{2,1,0:T(8,128)(2,1)S(1)}, bf16[1,16,256]{2,1,0:T(8,128)(2,1)S(1)}, u32[]{:S(2)}, u32[]{:S(2)}) collective-permute-start(bf16[1,16,256]{2,1,0:T(8,128)(2,1)S(1)} %get-tuple-element.13), channel_id=1, source_target_pairs={{16,32},{48,64},{80,96},{112,128},{144,160},{176,192},{208,224},{2... | collective-permute-start | bytes 24584 | tf_op jit(solution)/shard_map/ppermute | solution.py:276
  2.0 9.2 %collective-permute-start = (bf16[1,16,256]{2,1,0:T(8,128)(2,1)S(1)}, bf16[1,16,256]{2,1,0:T(8,128)(2,1)S(1)}, u32[]{:S(2)}, u32[]{:S(2)}) collective-permute-start(bf16[1,16,256]{2,1,0:T(8,128)(2,1)S(1)} %get-tuple-element.14), channel_id=1, source_target_pairs={{0,16},{32,48},{64,80},{96,112},{128,144},{160,176},{192,208},{224... | collective-permute-start | bytes 24584 | tf_op jit(solution)/shard_map/ppermute | solution.py:276
  11.2 8.8 %copy-start.3 = (bf16[1,16,256]{2,1,0:T(8,128)(2,1)}, bf16[1,16,256]{2,1,0:T(8,128)(2,1)S(1)}, u32[]{:S(2)}) copy-start(bf16[1,16,256]{2,1,0:T(8,128)(2,1)S(1)} %get-tuple-element.19.bottom_hbm) | copy-start | bytes 24580
  11.2 8.8 %copy-start.4 = (bf16[1,16,256]{2,1,0:T(8,128)(2,1)}, bf16[1,16,256]{2,1,0:T(8,128)(2,1)S(1)}, u32[]{:S(2)}) copy-start(bf16[1,16,256]{2,1,0:T(8,128)(2,1)S(1)} %get-tuple-element.20.top_hbm) | copy-start | bytes 24580
  11.4 6.9 %collective-permute-start.3 = (bf16[18,1,256]{2,1,0:T(2,128)(2,1)S(1)}, bf16[18,1,256]{2,1,0:T(2,128)(2,1)S(1)}, u32[]{:S(2)}, u32[]{:S(2)}) collective-permute-start(bf16[18,1,256]{2,1,0:T(2,128)(2,1)S(1)} %get-tuple-element.17), channel_id=1, source_target_pairs={{1,2},{3,4},{5,6},{7,8},{9,10},{11,12},{13,14},{2,1},{4,3},{6,5},{... | collective-permute-start | bytes 27656 | tf_op jit(solution)/shard_map/ppermute | solution.py:276
  16.3 3.1 %collective-permute-start.2 = (bf16[18,1,256]{2,1,0:T(2,128)(2,1)S(1)}, bf16[18,1,256]{2,1,0:T(2,128)(2,1)S(1)}, u32[]{:S(2)}, u32[]{:S(2)}) collective-permute-start(bf16[18,1,256]{2,1,0:T(2,128)(2,1)S(1)} %get-tuple-element.18), channel_id=1, source_target_pairs={{0,1},{2,3},{4,5},{6,7},{8,9},{10,11},{12,13},{14,15},{1,0},{3,2},... | collective-permute-start | bytes 27656 | tf_op jit(solution)/shard_map/ppermute | solution.py:276
  20.0 56.8 %copy-start = (bf16[256,256]{1,0:T(8,128)(2,1)S(1)}, bf16[256,256]{1,0:T(8,128)(2,1)}, u32[]{:S(2)}) copy-start(bf16[256,256]{1,0:T(8,128)(2,1)} %out_weight_ref.1) | copy-start | bytes 393220
  20.0 56.8 %copy-start.1 = (f32[100,256]{1,0:T(8,128)S(1)}, f32[100,256]{1,0:T(8,128)}, u32[]{:S(2)}) copy-start(f32[100,256]{1,0:T(8,128)} %queries_ref.1) | copy-start | bytes 307204
  20.1 56.8 %copy-start.2 = (f32[256]{0:T(256)S(1)}, f32[256]{0:T(256)}, u32[]{:S(2)}) copy-start(f32[256]{0:T(256)} %param.14) | copy-start | bytes 3076

commit v3 on v2

--- a/solution.py
+++ b/solution.py
@@ -24,7 +24,6 @@
 
 masked_low = -1e30
 tap_table = (((1, 1), (0, 3)), ((1, 2), (2, 0)))
-query_chunks = ((0, 40), (40, 32), (72, 32))
 
 
 def dot(a, b):
@@ -39,57 +38,73 @@
     return lax.broadcasted_iota(jnp.int32, shape, dim)
 
 
-def local_kernel(
-    x_hbm, top_hbm, bottom_hbm, left_hbm, right_hbm, weight_hbm, query_weight_hbm, kv_weight_hbm,
-    queries_hbm, named_hbm, pixels_hbm, part_hbm,
-    padded, left_ref, right_ref, weight_ref, query_weight_ref, kv_weight_ref, queries_ref, named_ref, pixels_ref, part_ref,
-    shifted, joined, wide_queries, keys, values, flags, spread, half_sums, half_side, arrived, sent
+def prepare_kernel(
+    x_hbm, weight_hbm, query_weight_hbm, kv_weight_hbm, queries_hbm, named_hbm,
+    x_ref, weight_ref, kv_weight_ref, wide_queries, flags,
+    query_weight_ref, queries_ref, named_ref, spread, arrived
 ):
-    def fetch(source, target, slot):
-        copy = pltpu.make_async_copy(source, target, arrived.at[slot])
+    copies = [
+        pltpu.make_async_copy(source, target, arrived.at[slot])
+        for slot, (source, target) in enumerate((
+            (queries_hbm, queries_ref), (query_weight_hbm, query_weight_ref), (named_hbm, named_ref),
+            (x_hbm, x_ref), (weight_hbm, weight_ref), (kv_weight_hbm, kv_weight_ref),
+        ))
+    ]
+    for copy in copies:
         copy.start()
-        return copy
-
-    fetch_queries = fetch(queries_hbm, queries_ref, 0)
-    fetch_query_weight = fetch(query_weight_hbm, query_weight_ref, 1)
-    fetch_named = fetch(named_hbm, named_ref, 2)
-    fetch_features = [
-        fetch(top_hbm, padded.at[pl.ds(0, 1)], 3),
-        fetch(x_hbm, padded.at[pl.ds(1, ROWS_IN)], 9),
-        fetch(bottom_hbm, padded.at[pl.ds(ROWS_IN + 1, 1)], 10),
-        fetch(left_hbm, left_ref, 11),
-        fetch(right_hbm, right_ref, 12),
-    ]
-    fetch_weight = {}
-    for a in range(2):
-        for _, row_kernel in tap_table[a]:
-            fetch_weight[row_kernel] = fetch(
-                weight_hbm.at[row_kernel], weight_ref.at[row_kernel], 4 + row_kernel
-            )
-        if a == 0:
-            fetch_kv_weight = fetch(kv_weight_hbm, kv_weight_ref, 8)
-
-    own_head = iota((1, HEADS, C), 2) // HEAD == iota((1, HEADS, C), 1)
-    fetch_queries.wait()
-    fetch_query_weight.wait()
+
+    copies[0].wait()
+    copies[1].wait()
     projected = dot(queries_ref[...].astype(jnp.bfloat16), query_weight_ref[...]) * HEAD ** (-0.5)
     spread[:QUERIES] = projected
     spread[QUERIES:] = jnp.zeros((PADDED - QUERIES, C), jnp.float32)
+    own_head = iota((1, HEADS, C), 2) // HEAD == iota((1, HEADS, C), 1)
     each = jnp.where(own_head, spread[...][:, None, :], 0.0)
     wide_queries[...] = each.reshape(PADDED * HEADS, C).astype(jnp.bfloat16)
 
-    fetch_named.wait()
+    copies[2].wait()
     block_id = lax.axis_index("rows") * lax.axis_size("cols") + lax.axis_index("cols")
     hits = (named_ref[...] == block_id).astype(jnp.bfloat16)
     flags[:QUERIES] = lax.dot_general(
-        hits, jnp.ones((hits.shape[0], LANES), jnp.bfloat16), (((0,), (0,)), ((), ())), preferred_element_type=jnp.float32
+        hits, jnp.ones((hits.shape[0], LANES), jnp.bfloat16), (((0,), (0,)), ((), ())),
+        preferred_element_type=jnp.float32,
     )
     flags[QUERIES:] = jnp.zeros((PADDED - QUERIES, LANES), jnp.float32)
-
-    for copy in fetch_features:
+    for copy in copies[3:]:
         copy.wait()
+
+
+def prepare(x, weight, query_weight, kv_weight, queries, active_blocks):
+    named = active_blocks.T
+    operands = [
+        pltpu.with_memory_space_constraint(t, pltpu.HBM)
+        for t in (x, weight, query_weight, kv_weight, queries, named)
+    ]
+    vmem = pl.BlockSpec(memory_space=pltpu.VMEM)
+    made = (
+        x, weight, kv_weight,
+        jax.ShapeDtypeStruct((PADDED * HEADS, C), jnp.bfloat16),
+        jax.ShapeDtypeStruct((PADDED, LANES), jnp.float32),
+    )
+    return pl.pallas_call(
+        prepare_kernel,
+        out_shape=tuple(jax.ShapeDtypeStruct(t.shape, t.dtype) for t in made),
+        in_specs=[pl.BlockSpec(memory_space=pltpu.HBM)] * len(operands),
+        out_specs=[vmem] * len(made),
+        scratch_shapes=[pltpu.VMEM(t.shape, t.dtype) for t in (query_weight, queries, named)]
+        + [pltpu.VMEM((PADDED, C), jnp.float32), pltpu.SemaphoreType.DMA((6,))],
+        compiler_params=pltpu.CompilerParams(vmem_limit_bytes=16 << 20),
+        cost_estimate=pl.CostEstimate(flops=20_000_000, bytes_accessed=6_000_000, transcendentals=0),
+    )(*operands)
+
+
+def local_kernel(
+    x_ref, top_ref, bottom_ref, left_ref, right_ref, weight_ref, kv_weight_ref, wide_queries, flags,
+    pixels_hbm, part_ref,
+    pixels_ref, shifted, joined, keys, values, half_sums, half_side, sent
+):
     height = ROWS_IN + 2
-    middle = padded[...]
+    middle = jnp.concatenate([top_ref[...], x_ref[...], bottom_ref[...]], axis=0)
     shifted[1] = middle.reshape(height * COLS_IN, C)
     middle = middle.astype(jnp.float32)
     column = iota((height, COLS_IN, C), 1)
@@ -102,10 +117,6 @@
 
     area = ROWS_IN * COLS_IN
     for a in range(2):
-        for _, row_kernel in tap_table[a]:
-            fetch_weight[row_kernel].wait()
-        if a == 0:
-            fetch_kv_weight.wait()
         for b in range(2):
             total = None
             for row_offset, row_kernel in tap_table[a]:
@@ -123,36 +134,34 @@
     for half in range(2):
         part = joined[half].reshape(2 * ROWS_IN, 2 * COLS_IN, LANES).astype(jnp.bfloat16)
         pixels_ref[:, :, half * LANES : (half + 1) * LANES] = part
-    send_pixels = pltpu.make_async_copy(pixels_ref, pixels_hbm, sent.at[0])
+    send_pixels = pltpu.make_async_copy(pixels_ref, pixels_hbm, sent)
     send_pixels.start()
 
     ones = jnp.ones((4 * area, LANES), jnp.bfloat16)
-    for start, count in query_chunks:
-        rows = slice(start * HEADS, (start + count) * HEADS)
-        now = lax.dot_general(
-            wide_queries[rows], keys[...], (((1,), (1,)), ((), ())), preferred_element_type=jnp.float32
-        )
-        highest = jnp.max(now, axis=1, keepdims=True)
-        weights = jnp.exp(now - highest).astype(jnp.bfloat16)
-        summed = dot(weights, values[...]).reshape(count, HEADS, C)
-        totals = dot(weights, ones).reshape(count, HEADS, LANES)
-        highest = jnp.broadcast_to(highest, (count * HEADS, LANES)).reshape(count, HEADS, LANES)
-        here = flags[start : start + count] > 0.0
-        summed = jnp.sum(jnp.where(own_head, summed, 0.0), axis=1)
-        lane = iota((count, HEADS, LANES), 2)
-        head = iota((count, HEADS, LANES), 1)
-        for half in range(2):
-            at = half * PADDED + start
-            into = slice(at, at + count)
-            half_sums[into] = jnp.where(here, summed[:, half * LANES : (half + 1) * LANES], 0.0)
-            row = lax.rem(iota((count, HEADS, LANES), 0) + at, SHARE)
-            slot = lane - TILE * row
-            own = head - HALF * half
-            own = jnp.where((own >= 0) & (own < HALF), own, -TILE * LANES)
-            is_highest = slot == own
-            placed = jnp.where(is_highest, highest, 0.0) + jnp.where(slot == own + HALF, totals, 0.0)
-            absent = jnp.sum(jnp.where(is_highest, masked_low, 0.0), axis=1)
-            half_side[into] = jnp.where(here, jnp.sum(placed, axis=1), absent)
+    own_head = iota((1, HEADS, C), 2) // HEAD == iota((1, HEADS, C), 1)
+    scores = lax.dot_general(
+        wide_queries[...], keys[...], (((1,), (1,)), ((), ())), preferred_element_type=jnp.float32
+    )
+    highest = jnp.max(scores, axis=1, keepdims=True)
+    weights = jnp.exp(scores - highest).astype(jnp.bfloat16)
+    summed = dot(weights, values[...]).reshape(PADDED, HEADS, C)
+    totals = dot(weights, ones).reshape(PADDED, HEADS, LANES)
+    highest = jnp.broadcast_to(highest, (PADDED * HEADS, LANES)).reshape(PADDED, HEADS, LANES)
+    here = flags[...] > 0.0
+    summed = jnp.sum(jnp.where(own_head, summed, 0.0), axis=1)
+    lane = iota((PADDED, HEADS, LANES), 2)
+    head = iota((PADDED, HEADS, LANES), 1)
+    for half in range(2):
+        into = slice(half * PADDED, (half + 1) * PADDED)
+        half_sums[into] = jnp.where(here, summed[:, half * LANES : (half + 1) * LANES], 0.0)
+        row = lax.rem(iota((PADDED, HEADS, LANES), 0) + half * PADDED, SHARE)
+        slot = lane - TILE * row
+        own = head - HALF * half
+        own = jnp.where((own >= 0) & (own < HALF), own, -TILE * LANES)
+        is_highest = slot == own
+        placed = jnp.where(is_highest, highest, 0.0) + jnp.where(slot == own + HALF, totals, 0.0)
+        absent = jnp.sum(jnp.where(is_highest, masked_low, 0.0), axis=1)
+        half_side[into] = jnp.where(here, jnp.sum(placed, axis=1), absent)
 
     for buffer in (half_sums, half_side):
         buffer[HALVES:] = jnp.zeros((buffer.shape[0] - HALVES, LANES), jnp.float32)
@@ -163,41 +172,31 @@
         part_ref[index, SHARE:] = jnp.sum(half_side[rows], axis=0, keepdims=True)
     if filled < part_ref.shape[0]:
         part_ref[filled:] = jnp.zeros((part_ref.shape[0] - filled, TILE, LANES), jnp.float32)
-    send_part = pltpu.make_async_copy(part_ref, part_hbm, sent.at[1])
-    send_part.start()
     send_pixels.wait()
-    send_part.wait()
-
-
-def local(x, top, bottom, left, right, weight, query_weight, kv_weight, queries, active_blocks, shares):
+
+
+def local(x, top, bottom, left, right, weight, kv_weight, wide_queries, flags, shares):
     area = ROWS_IN * COLS_IN
     pixels = jax.ShapeDtypeStruct((2 * ROWS_IN, 2 * COLS_IN, C), jnp.bfloat16)
-    padded = jax.ShapeDtypeStruct((ROWS_IN + 2, COLS_IN, C), jnp.bfloat16)
-    part = jax.ShapeDtypeStruct((shares, TILE, LANES), jnp.float32)
-    anywhere = pl.BlockSpec(memory_space=pl.ANY)
-    named = active_blocks.T
+    vmem = pl.BlockSpec(memory_space=pltpu.VMEM)
     return pl.pallas_call(
         local_kernel,
-        out_shape=(pixels, part),
-        in_specs=[anywhere] * 10,
-        out_specs=[anywhere] * 2,
-        scratch_shapes=[pltpu.VMEM(t.shape, t.dtype) for t in (padded, left, right, weight, query_weight, kv_weight, queries, named, pixels, part)]
-        + [
+        out_shape=(pixels, jax.ShapeDtypeStruct((shares, TILE, LANES), jnp.float32)),
+        in_specs=[vmem] * 9,
+        out_specs=[pl.BlockSpec(memory_space=pltpu.HBM), vmem],
+        scratch_shapes=[
+            pltpu.VMEM(pixels.shape, pixels.dtype),
             pltpu.VMEM((3, (ROWS_IN + 2) * COLS_IN, C), jnp.bfloat16),
             pltpu.VMEM((2, ROWS_IN, 2, 2 * COLS_IN, LANES), jnp.float32),
-            pltpu.VMEM((PADDED * HEADS, C), jnp.bfloat16),
             pltpu.VMEM((4 * area, C), jnp.bfloat16),
             pltpu.VMEM((4 * area, C), jnp.bfloat16),
-            pltpu.VMEM((PADDED, LANES), jnp.float32),
-            pltpu.VMEM((PADDED, C), jnp.float32),
             pltpu.VMEM((HALVES + TILE, LANES), jnp.float32),
             pltpu.VMEM((HALVES + TILE, LANES), jnp.float32),
-            pltpu.SemaphoreType.DMA((13,)),
-            pltpu.SemaphoreType.DMA((2,)),
+            pltpu.SemaphoreType.DMA,
         ],
-        compiler_params=pltpu.CompilerParams(vmem_limit_bytes=60 << 20),
+        compiler_params=pltpu.CompilerParams(vmem_limit_bytes=40 << 20),
         cost_estimate=pl.CostEstimate(flops=2_000_000_000, bytes_accessed=4_000_000, transcendentals=800_000),
-    )(x, top, bottom, left, right, weight, query_weight, kv_weight, queries, named)
+    )(x, top, bottom, left, right, weight, kv_weight, wide_queries, flags)
 
 
 def widened(side, first):
@@ -286,9 +285,10 @@
     )
     left, right = neighbours(edges, "cols", 1)
     row_peers, col_peers = lax.axis_size("rows"), lax.axis_size("cols")
-    pixels, part = local(
-        features, top, bottom, left, right, conv_weight, query_weight, kv_weight, queries, active_blocks, row_peers
-    )
+    x, weight, kv_weight, wide_queries, flags = prepare(
+        features, conv_weight, query_weight, kv_weight, queries, active_blocks
+    )
+    pixels, part = local(x, top, bottom, left, right, weight, kv_weight, wide_queries, flags, row_peers)
     parts = lax.all_to_all(part, "rows", 0, 0)
     copies = jax.ShapeDtypeStruct((col_peers, TILE, LANES), jnp.float32)
     parts = lax.all_to_all(on_device(merge_kernel, copies, parts), "cols", 0, 0)

time: 78.3 us -> 74.8 us (0.955)
  Pallas kernels: 8.55 us -> 7.38 us
  waiting for transfers between devices: 1.24 us -> 0.1 us
    pallas_call x1 -> x2, Pallas kernels: 6.93 us -> 5.76 us  [the longest x1 3.89 us: local(): pl.pallas_call(local_kernel, out_shape=(pixels, jax.ShapeDtypeStruct((sha...]
    ppermute x4, waiting for transfers between devices: 1.24 us -> 0.1 us  [neighbours(): swaps.append(lax.ppermute(edge, axis, pairs + [(j, i) for i, j in pairs]))]
  transfers between devices with their start and end apart: 4 -> 4, of which waited for: 2 -> 1; matrix products, arithmetic and copies ran while one was open for 1% -> 1% of each run, Pallas kernels for 0% -> 3%
where the time goes in v3:
time: 74.8 us; the launch traced here: 74.3 us
  blocking collectives  48.6 us (65%)
  starting transfers between devices  15.7 us (21%)
  Pallas kernels  7.38 us (10%)
  local copies, waits for them, and re-layouts  0.93 us (1%)
  other arithmetic  0.88 us (1%)
  between operations  0.79 us (1%)
    all_to_all x1, blocking collectives, body(): parts = lax.all_to_all(part, 'rows', 0, 0)  20.6 us
    all_to_all x1, blocking collectives, body(): parts = lax.all_to_all(on_device(merge_kernel, copies, parts), 'cols', 0, 0)  15.8 us
    ppermute x4, starting transfers between devices, neighbours(): swaps.append(lax.ppermute(edge, axis, pairs + [(j, i) for i, j in pairs]))  15.7 us
    all_to_all x1, blocking collectives, body(): lax.all_to_all(on_device(attend_kernel, copies, parts), 'rows', 0, 0)  12.2 us
    pallas_call x1, Pallas kernels, local(): pl.pallas_call(local_kernel, out_shape=(pixels, jax.ShapeDtypeStruct((sha...  3.89 us
    pallas_call x1, Pallas kernels, prepare(): pl.pallas_call(prepare_kernel, out_shape=tuple((jax.ShapeDtypeStruct(t.sh...  1.87 us
    pallas_call x3, Pallas kernels, on_device(): pl.pallas_call(kernel, out_shape=out_shape, in_specs=[pl.BlockSpec(memory...  1.62 us
  transfers between devices with their start and end apart: 4, of which 1 were waited for; matrix products, arithmetic and copies ran while one was open for 1% of the time, Pallas kernels for 3%

profile of v3, /device:TPU:1, one launch (start us, length us, event | category | flops | bytes accessed | tf_op | source)
XLA Modules:
  0.0 74.3 jit_solution(975305922296580761)
XLA Ops:
  0.6 0.7 broadcast_select_fusion.6
  1.4 0.6 collective-permute-start.1
  2.0 8.2 %collective-permute-start = (bf16[1,16,256]{2,1,0:T(8,128)(2,1)S(1)}, bf16[1,16,256]{2,1,0:T(8,128)(2,1)S(1)}, u32[]{:S(2)}, u32[]{:S(2)}) collective-permute-start(bf16[1,16,256]{2,1,0:T(8,128)(2,1)S(1)} %get-tuple-element.24), channel_id=1, source_target_pairs={{0,16},{32,48},{64,80},{96,112},{128,144},{160,176},{192,208},{224... | collective-permute-start | bytes 24584 | tf_op jit(solution)/shard_map/ppermute | solution.py:275
  10.2 0.9 %fusion = (bf16[16,1,256]{2,1,0:T(2,128)(2,1)S(1)}, bf16[16,1,256]{2,1,0:T(2,128)(2,1)S(1)}) fusion(bf16[16,16,256]{2,1,0:T(8,128)(2,1)} %x_hbm.1), kind=kLoop, calls=%fused_computation.9 | loop fusion | bytes 32768 | tf_op jit(solution)/shard_map/slice | solution.py:284
  11.1 0.0 collective-permute-done.1
  11.1 0.1 collective-permute-done
  11.4 4.9 %collective-permute-start.3 = (bf16[18,1,256]{2,1,0:T(2,128)(2,1)S(1)}, bf16[18,1,256]{2,1,0:T(2,128)(2,1)S(1)}, u32[]{:S(2)}, u32[]{:S(2)}) collective-permute-start(bf16[18,1,256]{2,1,0:T(2,128)(2,1)S(1)} %get-tuple-element.27), channel_id=1, source_target_pairs={{1,2},{3,4},{5,6},{7,8},{9,10},{11,12},{13,14},{2,1},{4,3},{6,5},{... | collective-permute-start | bytes 27656 | tf_op jit(solution)/shard_map/ppermute | solution.py:275
  16.3 1.9 %collective-permute-start.2 = (bf16[18,1,256]{2,1,0:T(2,128)(2,1)S(1)}, bf16[18,1,256]{2,1,0:T(2,128)(2,1)S(1)}, u32[]{:S(2)}, u32[]{:S(2)}) collective-permute-start(bf16[18,1,256]{2,1,0:T(2,128)(2,1)S(1)} %get-tuple-element.28), channel_id=1, source_target_pairs={{0,1},{2,3},{4,5},{6,7},{8,9},{10,11},{12,13},{14,15},{1,0},{3,2},... | collective-permute-start | bytes 27656 | tf_op jit(solution)/shard_map/ppermute | solution.py:275
  18.2 1.9 %shard_map.103 = (bf16[16,16,256]{2,1,0:T(8,128)(2,1)S(1)}, bf16[4,4,256,256]{3,2,1,0:T(8,128)(2,1)S(1)}, bf16[256,512]{1,0:T(8,128)(2,1)S(1)}, bf16[832,256]{1,0:T(8,128)(2,1)S(1)}, f32[104,128]{1,0:T(8,128)S(1)}) custom-call(bf16[16,16,256]{2,1,0:T(8,128)(2,1)} %x_hbm.1, bf16[4,4,256,256]{3,2,1,0:T(8,128)(2,1)} %weight_hbm.1, ...), custom_call_target="tpu_custom_call" | custom-call | flops 20000000 | bytes 6000000 | tf_op jit(solution)/shard_map/pallas_call | solution.py:89
  20.1 0.0 collective-permute-done.3
  20.1 0.0 collective-permute-done.2
  20.2 0.0 copy-start
  20.2 0.0 copy-start.1
  20.2 0.0 copy-start.2
  20.2 3.9 %shard_map.104 = (bf16[32,32,256]{2,1,0:T(8,128)(2,1)}, f32[32,8,128]{2,1,0:T(8,128)S(1)}) custom-call(bf16[16,16,256]{2,1,0:T(8,128)(2,1)S(1)} %get-tuple-element.12.x_ref, bf16[1,16,256]{2,1,0:T(8,128)(2,1)S(1)} %get-tuple-element.30.top_ref, bf16[1,16,256]{2,1,0:T(8,128)(2,1)S(1)} %get-tuple-element.29.bottom_ref, ...), custom_call_target="tpu_custom_call" | custom-call | flops 2000000000 | bytes 4000000 | tf_op jit(solution)/shard_map/pallas_call | solution.py:182
  24.1 20.6 %all_to_all.15.parts_ref = f32[32,8,128]{2,1,0:T(8,128)S(1)} all-to-all(f32[32,8,128]{2,1,0:T(8,128)S(1)} %get-tuple-element.18), channel_id=1, replica_groups=mesh['rows'=32,'cols'=16] {'rows'}, dimensions={0} | all-to-all | bytes 262144 | tf_op jit(solution)/shard_map/all_to_all | solution.py:292
  44.7 0.3 shard_map.105
  45.0 15.8 %all_to_all.16.parts_ref = f32[16,8,128]{2,1,0:T(8,128)S(1)} all-to-all(f32[16,8,128]{2,1,0:T(8,128)S(1)} %shard_map.105), channel_id=1, replica_groups=mesh['rows'=32,'cols'=16] {'cols'}, dimensions={0} | all-to-all | bytes 131072 | tf_op jit(solution)/shard_map/all_to_all | solution.py:294
  60.8 0.3 shard_map.106
  61.1 12.2 %all_to_all.17.attention_ref = bf16[32,8,128]{2,1,0:T(8,128)(2,1)S(1)} all-to-all(bf16[32,8,128]{2,1,0:T(8,128)(2,1)S(1)} %shard_map.106), channel_id=1, replica_groups=mesh['rows'=32,'cols'=16] {'rows'}, dimensions={0} | all-to-all | bytes 131072 | tf_op jit(solution)/shard_map/all_to_all | solution.py:296
  73.3 0.0 copy-done
  73.3 0.0 copy-done.1
  73.3 0.0 copy-done.2
  73.4 1.0 %shard_map.107 = (f32[100,256]{1,0:T(8,128)}, f32[100,256]{1,0:T(8,128)}) custom-call(bf16[32,8,128]{2,1,0:T(8,128)(2,1)S(1)} %all_to_all.17.attention_ref, bf16[256,256]{1,0:T(8,128)(2,1)S(1)} %copy-done.1, f32[100,256]{1,0:T(8,128)S(1)} %copy-done, f32[1,256]{1,0:T(1,128)S(1)} %bitcast.2), custom_call_target="tpu_custom_call" | custom-call | flops 10000000 | bytes 500000 | tf_op jit(solution)/shard_map/pallas_call | solution.py:256
  (5 shorter events, 0.2 us)
Async XLA Ops:
  1.4 9.8 %collective-permute-start.1 = (bf16[1,16,256]{2,1,0:T(8,128)(2,1)S(1)}, bf16[1,16,256]{2,1,0:T(8,128)(2,1)S(1)}, u32[]{:S(2)}, u32[]{:S(2)}) collective-permute-start(bf16[1,16,256]{2,1,0:T(8,128)(2,1)S(1)} %get-tuple-element.23), channel_id=1, source_target_pairs={{16,32},{48,64},{80,96},{112,128},{144,160},{176,192},{208,224},{2... | collective-permute-start | bytes 24584 | tf_op jit(solution)/shard_map/ppermute | solution.py:275
  2.0 9.2 %collective-permute-start = (bf16[1,16,256]{2,1,0:T(8,128)(2,1)S(1)}, bf16[1,16,256]{2,1,0:T(8,128)(2,1)S(1)}, u32[]{:S(2)}, u32[]{:S(2)}) collective-permute-start(bf16[1,16,256]{2,1,0:T(8,128)(2,1)S(1)} %get-tuple-element.24), channel_id=1, source_target_pairs={{0,16},{32,48},{64,80},{96,112},{128,144},{160,176},{192,208},{224... | collective-permute-start | bytes 24584 | tf_op jit(solution)/shard_map/ppermute | solution.py:275
  11.4 8.7 %collective-permute-start.3 = (bf16[18,1,256]{2,1,0:T(2,128)(2,1)S(1)}, bf16[18,1,256]{2,1,0:T(2,128)(2,1)S(1)}, u32[]{:S(2)}, u32[]{:S(2)}) collective-permute-start(bf16[18,1,256]{2,1,0:T(2,128)(2,1)S(1)} %get-tuple-element.27), channel_id=1, source_target_pairs={{1,2},{3,4},{5,6},{7,8},{9,10},{11,12},{13,14},{2,1},{4,3},{6,5},{... | collective-permute-start | bytes 27656 | tf_op jit(solution)/shard_map/ppermute | solution.py:275
  16.3 3.8 %collective-permute-start.2 = (bf16[18,1,256]{2,1,0:T(2,128)(2,1)S(1)}, bf16[18,1,256]{2,1,0:T(2,128)(2,1)S(1)}, u32[]{:S(2)}, u32[]{:S(2)}) collective-permute-start(bf16[18,1,256]{2,1,0:T(2,128)(2,1)S(1)} %get-tuple-element.28), channel_id=1, source_target_pairs={{0,1},{2,3},{4,5},{6,7},{8,9},{10,11},{12,13},{14,15},{1,0},{3,2},... | collective-permute-start | bytes 27656 | tf_op jit(solution)/shard_map/ppermute | solution.py:275
  20.2 53.2 %copy-start = (f32[100,256]{1,0:T(8,128)S(1)}, f32[100,256]{1,0:T(8,128)}, u32[]{:S(2)}) copy-start(f32[100,256]{1,0:T(8,128)} %queries_ref.1) | copy-start | bytes 307204
  20.2 53.2 %copy-start.1 = (bf16[256,256]{1,0:T(8,128)(2,1)S(1)}, bf16[256,256]{1,0:T(8,128)(2,1)}, u32[]{:S(2)}) copy-start(bf16[256,256]{1,0:T(8,128)(2,1)} %out_weight_ref.1) | copy-start | bytes 393220
  20.2 53.2 %copy-start.2 = (f32[256]{0:T(256)S(1)}, f32[256]{0:T(256)}, u32[]{:S(2)}) copy-start(f32[256]{0:T(256)} %param.14) | copy-start | bytes 3076

commit v4 on v3

--- a/solution.py
+++ b/solution.py
@@ -39,7 +39,7 @@
 
 
 def prepare_kernel(
-    x_hbm, weight_hbm, query_weight_hbm, kv_weight_hbm, queries_hbm, named_hbm,
+    after, x_hbm, weight_hbm, query_weight_hbm, kv_weight_hbm, queries_hbm, named_hbm,
     x_ref, weight_ref, kv_weight_ref, wide_queries, flags,
     query_weight_ref, queries_ref, named_ref, spread, arrived
 ):
@@ -74,7 +74,7 @@
         copy.wait()
 
 
-def prepare(x, weight, query_weight, kv_weight, queries, active_blocks):
+def prepare(after, x, weight, query_weight, kv_weight, queries, active_blocks):
     named = active_blocks.T
     operands = [
         pltpu.with_memory_space_constraint(t, pltpu.HBM)
@@ -89,41 +89,77 @@
     return pl.pallas_call(
         prepare_kernel,
         out_shape=tuple(jax.ShapeDtypeStruct(t.shape, t.dtype) for t in made),
-        in_specs=[pl.BlockSpec(memory_space=pltpu.HBM)] * len(operands),
+        in_specs=[pl.BlockSpec(memory_space=pl.ANY)] + [pl.BlockSpec(memory_space=pltpu.HBM)] * len(operands),
         out_specs=[vmem] * len(made),
         scratch_shapes=[pltpu.VMEM(t.shape, t.dtype) for t in (query_weight, queries, named)]
         + [pltpu.VMEM((PADDED, C), jnp.float32), pltpu.SemaphoreType.DMA((6,))],
         compiler_params=pltpu.CompilerParams(vmem_limit_bytes=16 << 20),
         cost_estimate=pl.CostEstimate(flops=20_000_000, bytes_accessed=6_000_000, transcendentals=0),
-    )(*operands)
-
-
-def local_kernel(
-    x_ref, top_ref, bottom_ref, left_ref, right_ref, weight_ref, kv_weight_ref, wide_queries, flags,
-    pixels_hbm, part_ref,
-    pixels_ref, shifted, joined, keys, values, half_sums, half_side, sent
-):
-    height = ROWS_IN + 2
-    middle = jnp.concatenate([top_ref[...], x_ref[...], bottom_ref[...]], axis=0)
-    shifted[1] = middle.reshape(height * COLS_IN, C)
-    middle = middle.astype(jnp.float32)
-    column = iota((height, COLS_IN, C), 1)
+    )(after, *operands)
+
+
+def middle_kernel(x_ref, left_ref, right_ref, weight_ref, shifted, totals):
+    area = ROWS_IN * COLS_IN
+    shifted[1] = x_ref[...].reshape(area, C)
+    x = x_ref[...].astype(jnp.float32)
+    column = iota((ROWS_IN, COLS_IN, C), 1)
     left = left_ref[...].astype(jnp.float32)
     right = right_ref[...].astype(jnp.float32)
-    before = jnp.where(column == 0, left, pltpu.roll(middle, 1, 1))
-    after = jnp.where(column == COLS_IN - 1, right, pltpu.roll(middle, COLS_IN - 1, 1))
-    shifted[0] = before.astype(jnp.bfloat16).reshape(height * COLS_IN, C)
-    shifted[2] = after.astype(jnp.bfloat16).reshape(height * COLS_IN, C)
-
-    area = ROWS_IN * COLS_IN
+    before = jnp.where(column == 0, left, pltpu.roll(x, 1, 1))
+    after = jnp.where(column == COLS_IN - 1, right, pltpu.roll(x, COLS_IN - 1, 1))
+    shifted[0] = before.astype(jnp.bfloat16).reshape(area, C)
+    shifted[2] = after.astype(jnp.bfloat16).reshape(area, C)
     for a in range(2):
         for b in range(2):
             total = None
             for row_offset, row_kernel in tap_table[a]:
-                for col_offset, col_kernel in tap_table[b]:
-                    window = shifted[col_offset, row_offset * COLS_IN : row_offset * COLS_IN + area]
-                    term = dot(window, weight_ref[row_kernel, col_kernel])
-                    total = term if total is None else total + term
+                if row_offset == 1:
+                    for col_offset, col_kernel in tap_table[b]:
+                        term = dot(shifted[col_offset], weight_ref[row_kernel, col_kernel])
+                        total = term if total is None else total + term
+            totals[2 * a + b] = total
+
+
+def middle(x, left, right, weight):
+    vmem = pl.BlockSpec(memory_space=pltpu.VMEM)
+    area = ROWS_IN * COLS_IN
+    return pl.pallas_call(
+        middle_kernel,
+        out_shape=(
+            jax.ShapeDtypeStruct((3, area, C), jnp.bfloat16),
+            jax.ShapeDtypeStruct((4, area, C), jnp.float32),
+        ),
+        in_specs=[vmem] * 4,
+        out_specs=[vmem] * 2,
+        compiler_params=pltpu.CompilerParams(vmem_limit_bytes=16 << 20),
+        cost_estimate=pl.CostEstimate(flops=270_000_000, bytes_accessed=3_000_000, transcendentals=0),
+    )(x, left, right, weight)
+
+
+def local_kernel(
+    top_ref, bottom_ref, shifted_ref, totals_ref, weight_ref, kv_weight_ref, wide_queries, flags,
+    pixels_hbm, part_ref,
+    pixels_ref, shifted, joined, keys, values, half_sums, half_side, sent
+):
+    area = ROWS_IN * COLS_IN
+    shifted[:, COLS_IN : COLS_IN + area] = shifted_ref[...]
+    for edge_ref, at in ((top_ref, 0), (bottom_ref, COLS_IN + area)):
+        edge = edge_ref[0].astype(jnp.float32)
+        row, left, right = edge[:COLS_IN], edge[COLS_IN : COLS_IN + 1], edge[COLS_IN + 1 :]
+        column = iota((COLS_IN, C), 0)
+        into = slice(at, at + COLS_IN)
+        shifted[0, into] = jnp.where(column == 0, left, pltpu.roll(row, 1, 0)).astype(jnp.bfloat16)
+        shifted[1, into] = row.astype(jnp.bfloat16)
+        shifted[2, into] = jnp.where(column == COLS_IN - 1, right, pltpu.roll(row, COLS_IN - 1, 0)).astype(jnp.bfloat16)
+
+    for a in range(2):
+        for b in range(2):
+            total = totals_ref[2 * a + b]
+            for row_offset, row_kernel in tap_table[a]:
+                if row_offset != 1:
+                    for col_offset, col_kernel in tap_table[b]:
+                        window = shifted[col_offset, row_offset * COLS_IN : row_offset * COLS_IN + area]
+                        total = total + dot(window, weight_ref[row_kernel, col_kernel])
             for half in range(2):
                 part = total[:, half * LANES : (half + 1) * LANES].reshape(ROWS_IN, COLS_IN, LANES)
                 joined[half, :, a, pl.ds(b, COLS_IN, stride=2), :] = part
@@ -175,14 +211,14 @@
     send_pixels.wait()
 
 
-def local(x, top, bottom, left, right, weight, kv_weight, wide_queries, flags, shares):
+def local(top, bottom, shifted, totals, weight, kv_weight, wide_queries, flags, shares):
     area = ROWS_IN * COLS_IN
     pixels = jax.ShapeDtypeStruct((2 * ROWS_IN, 2 * COLS_IN, C), jnp.bfloat16)
     vmem = pl.BlockSpec(memory_space=pltpu.VMEM)
     return pl.pallas_call(
         local_kernel,
         out_shape=(pixels, jax.ShapeDtypeStruct((shares, TILE, LANES), jnp.float32)),
-        in_specs=[vmem] * 9,
+        in_specs=[vmem] * 8,
         out_specs=[pl.BlockSpec(memory_space=pltpu.HBM), vmem],
         scratch_shapes=[
             pltpu.VMEM(pixels.shape, pixels.dtype),
@@ -196,7 +232,7 @@
         ],
         compiler_params=pltpu.CompilerParams(vmem_limit_bytes=40 << 20),
         cost_estimate=pl.CostEstimate(flops=2_000_000_000, bytes_accessed=4_000_000, transcendentals=800_000),
-    )(x, top, bottom, left, right, weight, kv_weight, wide_queries, flags)
+    )(top, bottom, shifted, totals, weight, kv_weight, wide_queries, flags)
 
 
 def widened(side, first):
@@ -264,31 +300,33 @@
     )(*operands)
 
 
-def neighbours(x, axis, dim):
+def swaps(first, last, axis):
     peers = lax.axis_size(axis)
-    last = lax.slice_in_dim(x, x.shape[dim] - 1, x.shape[dim], axis=dim)
-    first = lax.slice_in_dim(x, 0, 1, axis=dim)
     odd = lax.axis_index(axis) % 2 == 1
-    swaps = []
-    for start, edge in ((0, jnp.where(odd, first, last)), (1, jnp.where(odd, last, first))):
+    swapped = {}
+    for start, edge in ((1, jnp.where(odd, last, first)), (0, jnp.where(odd, first, last))):
         pairs = [(i, i + 1) for i in range(start, peers - 1, 2)]
-        swaps.append(lax.ppermute(edge, axis, pairs + [(j, i) for i, j in pairs]))
-    return jnp.where(odd, swaps[0], swaps[1]), jnp.where(odd, swaps[1], swaps[0])
+        swapped[start] = lax.ppermute(edge, axis, pairs + [(j, i) for i, j in pairs])
+    if axis == 'rows':
+        return jnp.where(odd, swapped[0], swapped[1]), jnp.where(odd, swapped[1], swapped[0])
+    even = jnp.logical_not(odd)
+    return jnp.where(even, swapped[1], swapped[0]), jnp.where(even, swapped[0], swapped[1])
 
 
 def body(
     features, conv_weight, query_weight, kv_weight, out_weight, queries, norm_gain, active_blocks
 ):
-    top, bottom = neighbours(features, "rows", 0)
-    edges = jnp.concatenate(
-        [jnp.concatenate([part[:, :1], part[:, -1:]], axis=1) for part in (top, features, bottom)], axis=0
-    )
-    left, right = neighbours(edges, "cols", 1)
+    left, right = swaps(features[:, :1], features[:, -1:], "cols")
+    first, last = [
+        jnp.concatenate([part[at : at + 1] for part in (features, left, right)], axis=1) for at in (0, ROWS_IN - 1)
+    ]
+    top, bottom = swaps(first, last, "rows")
+    x, weight, kv_weight, wide_queries, flags = prepare(
+        left, features, conv_weight, query_weight, kv_weight, queries, active_blocks
+    )
     row_peers, col_peers = lax.axis_size("rows"), lax.axis_size("cols")
-    x, weight, kv_weight, wide_queries, flags = prepare(
-        features, conv_weight, query_weight, kv_weight, queries, active_blocks
-    )
-    pixels, part = local(x, top, bottom, left, right, weight, kv_weight, wide_queries, flags, row_peers)
+    shifted, totals = middle(x, left, right, weight)
+    pixels, part = local(top, bottom, shifted, totals, weight, kv_weight, wide_queries, flags, row_peers)
     parts = lax.all_to_all(part, "rows", 0, 0)
     copies = jax.ShapeDtypeStruct((col_peers, TILE, LANES), jnp.float32)
     parts = lax.all_to_all(on_device(merge_kernel, copies, parts), "cols", 0, 0)

time: 74.8 us -> 73.6 us (0.984)
  starting transfers between devices: 15.7 us -> 14.8 us
    pallas_call x1, Pallas kernels: 3.89 us -> 2.82 us  [local(): pl.pallas_call(local_kernel, out_shape=(pixels, jax.ShapeDtypeStruct((sha...]
    all_to_all x1, blocking collectives: 15.8 us -> 16.9 us  [body(): parts = lax.all_to_all(on_device(merge_kernel, copies, parts), 'cols', 0, 0)]
    ppermute x4, starting transfers between devices: 15.7 us -> 14.8 us  [swaps(): lax.ppermute(edge, axis, pairs + [(j, i) for i, j in pairs])]
where the time goes in v4:
time: 73.6 us; the launch traced here: 73.2 us
  blocking collectives  48.9 us (66%)
  starting transfers between devices  14.8 us (20%)
  Pallas kernels  6.76 us (9%)
  other arithmetic  0.98 us (1%)
  between operations  0.78 us (1%)
  local copies, waits for them, and re-layouts  0.75 us (1%)
    all_to_all x1, blocking collectives, body(): parts = lax.all_to_all(part, 'rows', 0, 0)  20 us
    all_to_all x1, blocking collectives, body(): parts = lax.all_to_all(on_device(merge_kernel, copies, parts), 'cols', 0, 0)  16.9 us
    ppermute x4, starting transfers between devices, swaps(): lax.ppermute(edge, axis, pairs + [(j, i) for i, j in pairs])  14.8 us
    all_to_all x1, blocking collectives, body(): lax.all_to_all(on_device(attend_kernel, copies, parts), 'rows', 0, 0)  12.1 us
    pallas_call x1, Pallas kernels, local(): pl.pallas_call(local_kernel, out_shape=(pixels, jax.ShapeDtypeStruct((sha...  2.82 us
    pallas_call x1, Pallas kernels, prepare(): pl.pallas_call(prepare_kernel, out_shape=tuple((jax.ShapeDtypeStruct(t.sh...  1.87 us
    pallas_call x3, Pallas kernels, on_device(): pl.pallas_call(kernel, out_shape=out_shape, in_specs=[pl.BlockSpec(memory...  1.62 us
  transfers between devices with their start and end apart: 4, of which 1 were waited for; matrix products, arithmetic and copies ran while one was open for 1% of the time, Pallas kernels for 3%

profile of v4, /device:TPU:1, one launch (start us, length us, event | category | flops | bytes accessed | tf_op | source)
XLA Modules:
  0.0 73.2 jit_solution(6647128321389753215)
XLA Ops:
  0.6 0.9 %broadcast_select_fusion.1 = (bf16[16,1,256]{2,1,0:T(2,128)(2,1)S(1)}, bf16[16,1,256]{2,1,0:T(2,128)(2,1)S(1)}) fusion(pred[]{:T(512)S(6)} %eq.10, bf16[16,16,256]{2,1,0:T(8,128)(2,1)} %x_hbm.1), kind=kLoop, calls=%fused_computation.1 | loop fusion | flops 8192 | bytes 32769 | tf_op jit(solution)/shard_map/jit(_where)/select_n | solution.py:307
  1.6 4.6 %collective-permute-start = (bf16[16,1,256]{2,1,0:T(2,128)(2,1)S(1)}, bf16[16,1,256]{2,1,0:T(2,128)(2,1)S(1)}, u32[]{:S(2)}, u32[]{:S(2)}) collective-permute-start(bf16[16,1,256]{2,1,0:T(2,128)(2,1)S(1)} %get-tuple-element.27), channel_id=1, source_target_pairs={{1,2},{3,4},{5,6},{7,8},{9,10},{11,12},{13,14},{2,1},{4,3},{6,5},{... | collective-permute-start | bytes 24584 | tf_op jit(solution)/shard_map/ppermute | solution.py:309
  6.2 4.9 %collective-permute-start.1 = (bf16[16,1,256]{2,1,0:T(2,128)(2,1)S(1)}, bf16[16,1,256]{2,1,0:T(2,128)(2,1)S(1)}, u32[]{:S(2)}, u32[]{:S(2)}) collective-permute-start(bf16[16,1,256]{2,1,0:T(2,128)(2,1)S(1)} %get-tuple-element.28), channel_id=1, source_target_pairs={{0,1},{2,3},{4,5},{6,7},{8,9},{10,11},{12,13},{14,15},{1,0},{3,2},... | collective-permute-start | bytes 24584 | tf_op jit(solution)/shard_map/ppermute | solution.py:309
  11.0 0.7 fusion
  11.8 0.0 collective-permute-done
  11.8 0.1 collective-permute-done.1
  11.9 0.7 collective-permute-start.3
  12.6 4.7 %collective-permute-start.2 = (bf16[1,18,256]{2,1,0:T(8,128)(2,1)S(1)}, bf16[1,18,256]{2,1,0:T(8,128)(2,1)S(1)}, u32[]{:S(2)}, u32[]{:S(2)}) collective-permute-start(bf16[1,18,256]{2,1,0:T(8,128)(2,1)S(1)} %get-tuple-element.34), channel_id=1, source_target_pairs={{0,16},{32,48},{64,80},{96,112},{128,144},{160,176},{192,208},{224... | collective-permute-start | bytes 27656 | tf_op jit(solution)/shard_map/ppermute | solution.py:309
  17.3 1.9 %shard_map.103 = (bf16[16,16,256]{2,1,0:T(8,128)(2,1)S(1)}, bf16[4,4,256,256]{3,2,1,0:T(8,128)(2,1)S(1)}, bf16[256,512]{1,0:T(8,128)(2,1)S(1)}, bf16[832,256]{1,0:T(8,128)(2,1)S(1)}, f32[104,128]{1,0:T(8,128)S(1)}) custom-call(bf16[16,1,256]{2,1,0:T(2,128)(2,1)S(1)} %get-tuple-element.29.after.left_ref, bf16[16,16,256]{2,1,0:T(8,128)(2,1)} %x_hbm.1, ...), custom_call_target="tpu_custom_call" | custom-call | flops 20000000 | bytes 6000000 | tf_op jit(solution)/shard_map/pallas_call | solution.py:89
  19.2 0.5 shard_map.104
  19.7 0.0 collective-permute-done.3
  19.7 0.0 collective-permute-done.2
  19.7 0.0 copy-start
  19.7 0.0 copy-start.1
  19.7 0.0 copy-start.2
  19.7 2.8 %shard_map.105 = (bf16[32,32,256]{2,1,0:T(8,128)(2,1)}, f32[32,8,128]{2,1,0:T(8,128)S(1)}) custom-call(bf16[1,18,256]{2,1,0:T(8,128)(2,1)S(1)} %get-tuple-element.32.top_ref, bf16[1,18,256]{2,1,0:T(8,128)(2,1)S(1)} %get-tuple-element.31.bottom_ref, bf16[3,256,256]{2,1,0:T(8,128)(2,1)S(1)} %get-tuple-element.16.shifted_ref, ...), custom_call_target="tpu_custom_call" | custom-call | flops 2000000000 | bytes 4000000 | tf_op jit(solution)/shard_map/pallas_call | solution.py:218
  22.6 20.0 %all_to_all.15.parts_ref = f32[32,8,128]{2,1,0:T(8,128)S(1)} all-to-all(f32[32,8,128]{2,1,0:T(8,128)S(1)} %get-tuple-element.22), channel_id=1, replica_groups=mesh['rows'=32,'cols'=16] {'rows'}, dimensions={0} | all-to-all | bytes 262144 | tf_op jit(solution)/shard_map/all_to_all | solution.py:330
  42.6 0.3 shard_map.106
  42.9 16.9 %all_to_all.16.parts_ref = f32[16,8,128]{2,1,0:T(8,128)S(1)} all-to-all(f32[16,8,128]{2,1,0:T(8,128)S(1)} %shard_map.106), channel_id=1, replica_groups=mesh['rows'=32,'cols'=16] {'cols'}, dimensions={0} | all-to-all | bytes 131072 | tf_op jit(solution)/shard_map/all_to_all | solution.py:332
  59.8 0.3 shard_map.107
  60.1 12.1 %all_to_all.17.attention_ref = bf16[32,8,128]{2,1,0:T(8,128)(2,1)S(1)} all-to-all(bf16[32,8,128]{2,1,0:T(8,128)(2,1)S(1)} %shard_map.107), channel_id=1, replica_groups=mesh['rows'=32,'cols'=16] {'rows'}, dimensions={0} | all-to-all | bytes 131072 | tf_op jit(solution)/shard_map/all_to_all | solution.py:334
  72.2 0.0 copy-done
  72.2 0.0 copy-done.1
  72.2 0.0 copy-done.2
  72.2 1.0 %shard_map.108 = (f32[100,256]{1,0:T(8,128)}, f32[100,256]{1,0:T(8,128)}) custom-call(bf16[32,8,128]{2,1,0:T(8,128)(2,1)S(1)} %all_to_all.17.attention_ref, bf16[256,256]{1,0:T(8,128)(2,1)S(1)} %copy-done.1, f32[100,256]{1,0:T(8,128)S(1)} %copy-done, f32[1,256]{1,0:T(1,128)S(1)} %bitcast.2), custom_call_target="tpu_custom_call" | custom-call | flops 10000000 | bytes 500000 | tf_op jit(solution)/shard_map/pallas_call | solution.py:292
  (4 shorter events, 0.1 us)
Async XLA Ops:
  1.6 10.2 %collective-permute-start = (bf16[16,1,256]{2,1,0:T(2,128)(2,1)S(1)}, bf16[16,1,256]{2,1,0:T(2,128)(2,1)S(1)}, u32[]{:S(2)}, u32[]{:S(2)}) collective-permute-start(bf16[16,1,256]{2,1,0:T(2,128)(2,1)S(1)} %get-tuple-element.27), channel_id=1, source_target_pairs={{1,2},{3,4},{5,6},{7,8},{9,10},{11,12},{13,14},{2,1},{4,3},{6,5},{... | collective-permute-start | bytes 24584 | tf_op jit(solution)/shard_map/ppermute | solution.py:309
  6.2 5.7 %collective-permute-start.1 = (bf16[16,1,256]{2,1,0:T(2,128)(2,1)S(1)}, bf16[16,1,256]{2,1,0:T(2,128)(2,1)S(1)}, u32[]{:S(2)}, u32[]{:S(2)}) collective-permute-start(bf16[16,1,256]{2,1,0:T(2,128)(2,1)S(1)} %get-tuple-element.28), channel_id=1, source_target_pairs={{0,1},{2,3},{4,5},{6,7},{8,9},{10,11},{12,13},{14,15},{1,0},{3,2},... | collective-permute-start | bytes 24584 | tf_op jit(solution)/shard_map/ppermute | solution.py:309
  11.9 7.8 %collective-permute-start.3 = (bf16[1,18,256]{2,1,0:T(8,128)(2,1)S(1)}, bf16[1,18,256]{2,1,0:T(8,128)(2,1)S(1)}, u32[]{:S(2)}, u32[]{:S(2)}) collective-permute-start(bf16[1,18,256]{2,1,0:T(8,128)(2,1)S(1)} %get-tuple-element.33), channel_id=1, source_target_pairs={{16,32},{48,64},{80,96},{112,128},{144,160},{176,192},{208,224},{2... | collective-permute-start | bytes 27656 | tf_op jit(solution)/shard_map/ppermute | solution.py:309
  12.6 7.1 %collective-permute-start.2 = (bf16[1,18,256]{2,1,0:T(8,128)(2,1)S(1)}, bf16[1,18,256]{2,1,0:T(8,128)(2,1)S(1)}, u32[]{:S(2)}, u32[]{:S(2)}) collective-permute-start(bf16[1,18,256]{2,1,0:T(8,128)(2,1)S(1)} %get-tuple-element.34), channel_id=1, source_target_pairs={{0,16},{32,48},{64,80},{96,112},{128,144},{160,176},{192,208},{224... | collective-permute-start | bytes 27656 | tf_op jit(solution)/shard_map/ppermute | solution.py:309
  19.7 52.4 %copy-start = (f32[100,256]{1,0:T(8,128)S(1)}, f32[100,256]{1,0:T(8,128)}, u32[]{:S(2)}) copy-start(f32[100,256]{1,0:T(8,128)} %queries_ref.1) | copy-start | bytes 307204
  19.7 52.4 %copy-start.1 = (bf16[256,256]{1,0:T(8,128)(2,1)S(1)}, bf16[256,256]{1,0:T(8,128)(2,1)}, u32[]{:S(2)}) copy-start(bf16[256,256]{1,0:T(8,128)(2,1)} %out_weight_ref.1) | copy-start | bytes 393220
  19.7 52.4 %copy-start.2 = (f32[256]{0:T(256)S(1)}, f32[256]{0:T(256)}, u32[]{:S(2)}) copy-start(f32[256]{0:T(256)} %param.14) | copy-start | bytes 3076

commit v5 on v4

--- a/solution.py
+++ b/solution.py
@@ -22,6 +22,8 @@
 TILE = 8
 HALVES = 2 * PADDED
 
+sizes = (16, 32, 48, PADDED)
+
 masked_low = -1e30
 tap_table = (((1, 1), (0, 3)), ((1, 2), (2, 0)))
 
@@ -40,8 +42,8 @@
 
 def prepare_kernel(
     after, x_hbm, weight_hbm, query_weight_hbm, kv_weight_hbm, queries_hbm, named_hbm,
-    x_ref, weight_ref, kv_weight_ref, wide_queries, flags,
-    query_weight_ref, queries_ref, named_ref, spread, arrived
+    x_ref, weight_ref, kv_weight_ref, wide_queries, places,
+    query_weight_ref, queries_ref, named_ref, spread, flags, arrived
 ):
     copies = [
         pltpu.make_async_copy(source, target, arrived.at[slot])
@@ -58,9 +60,6 @@
     projected = dot(queries_ref[...].astype(jnp.bfloat16), query_weight_ref[...]) * HEAD ** (-0.5)
     spread[:QUERIES] = projected
     spread[QUERIES:] = jnp.zeros((PADDED - QUERIES, C), jnp.float32)
-    own_head = iota((1, HEADS, C), 2) // HEAD == iota((1, HEADS, C), 1)
-    each = jnp.where(own_head, spread[...][:, None, :], 0.0)
-    wide_queries[...] = each.reshape(PADDED * HEADS, C).astype(jnp.bfloat16)
 
     copies[2].wait()
     block_id = lax.axis_index("rows") * lax.axis_size("cols") + lax.axis_index("cols")
@@ -70,6 +69,18 @@
         preferred_element_type=jnp.float32,
     )
     flags[QUERIES:] = jnp.zeros((PADDED - QUERIES, LANES), jnp.float32)
+    active = flags[...] > 0.0
+    earlier = (iota((PADDED, PADDED), 1) < iota((PADDED, PADDED), 0)).astype(jnp.bfloat16)
+    rank = dot(earlier, active.astype(jnp.bfloat16)).astype(jnp.int32)
+    place = (active & (rank == iota((PADDED, LANES), 1))).astype(jnp.bfloat16)
+    places[...] = place.astype(jnp.float32)
+
+    chosen = lax.dot_general(
+        place, spread[...].astype(jnp.bfloat16), (((0,), (0,)), ((), ())), preferred_element_type=jnp.float32
+    )
+    own_head = iota((1, HEADS, C), 2) // HEAD == iota((1, HEADS, C), 1)
+    each = jnp.where(own_head, chosen[:PADDED][:, None, :], 0.0)
+    wide_queries[...] = each.reshape(PADDED * HEADS, C).astype(jnp.bfloat16)
     for copy in copies[3:]:
         copy.wait()
 
@@ -92,7 +103,11 @@
         in_specs=[pl.BlockSpec(memory_space=pl.ANY)] + [pl.BlockSpec(memory_space=pltpu.HBM)] * len(operands),
         out_specs=[vmem] * len(made),
         scratch_shapes=[pltpu.VMEM(t.shape, t.dtype) for t in (query_weight, queries, named)]
-        + [pltpu.VMEM((PADDED, C), jnp.float32), pltpu.SemaphoreType.DMA((6,))],
+        + [
+            pltpu.VMEM((PADDED, C), jnp.float32),
+            pltpu.VMEM((PADDED, LANES), jnp.float32),
+            pltpu.SemaphoreType.DMA((6,)),
+        ],
         compiler_params=pltpu.CompilerParams(vmem_limit_bytes=16 << 20),
         cost_estimate=pl.CostEstimate(flops=20_000_000, bytes_accessed=6_000_000, transcendentals=0),
     )(after, *operands)
@@ -137,9 +152,9 @@
 
 
 def local_kernel(
-    top_ref, bottom_ref, shifted_ref, totals_ref, weight_ref, kv_weight_ref, wide_queries, flags,
+    top_ref, bottom_ref, shifted_ref, totals_ref, weight_ref, kv_weight_ref, wide_queries, places,
     pixels_hbm, part_ref,
-    pixels_ref, shifted, joined, keys, values, half_sums, half_side, sent
+    pixels_ref, shifted, joined, keys, values, chosen, half_sums, half_side, sent
 ):
     area = ROWS_IN * COLS_IN
     shifted[:, COLS_IN : COLS_IN + area] = shifted_ref[...]
@@ -173,31 +188,50 @@
     send_pixels = pltpu.make_async_copy(pixels_ref, pixels_hbm, sent)
     send_pixels.start()
 
-    ones = jnp.ones((4 * area, LANES), jnp.bfloat16)
-    own_head = iota((1, HEADS, C), 2) // HEAD == iota((1, HEADS, C), 1)
-    scores = lax.dot_general(
-        wide_queries[...], keys[...], (((1,), (1,)), ((), ())), preferred_element_type=jnp.float32
-    )
-    highest = jnp.max(scores, axis=1, keepdims=True)
-    weights = jnp.exp(scores - highest).astype(jnp.bfloat16)
-    summed = dot(weights, values[...]).reshape(PADDED, HEADS, C)
-    totals = dot(weights, ones).reshape(PADDED, HEADS, LANES)
-    highest = jnp.broadcast_to(highest, (PADDED * HEADS, LANES)).reshape(PADDED, HEADS, LANES)
-    here = flags[...] > 0.0
-    summed = jnp.sum(jnp.where(own_head, summed, 0.0), axis=1)
-    lane = iota((PADDED, HEADS, LANES), 2)
-    head = iota((PADDED, HEADS, LANES), 1)
+    number = jnp.sum(places[...])
+
+    def attend(size):
+        scores = lax.dot_general(
+            wide_queries[: size * HEADS], keys[...], (((1,), (1,)), ((), ())), preferred_element_type=jnp.float32
+        )
+        highest = jnp.max(scores, axis=1, keepdims=True)
+        weights = jnp.exp(scores - highest).astype(jnp.bfloat16)
+        summed = dot(weights, values[...]).reshape(size, HEADS, C)
+        ones = jnp.ones((4 * area, LANES), jnp.bfloat16)
+        totals = dot(weights, ones).reshape(size, HEADS, LANES)
+        highest = jnp.broadcast_to(highest, (size * HEADS, LANES)).reshape(size, HEADS, LANES)
+        own_head = iota((1, HEADS, C), 2) // HEAD == iota((1, HEADS, C), 1)
+        chosen[:size, :C] = jnp.sum(jnp.where(own_head, summed, 0.0), axis=1)
+        lane = iota((1, HEADS, LANES), 2) % TILE
+        head = iota((1, HEADS, LANES), 1)
+        for half in range(2):
+            own = head - HALF * half
+            own = jnp.where((own >= 0) & (own < HALF), own, -TILE)
+            side = jnp.where(lane == own, highest, 0.0) + jnp.where(lane == own + HALF, totals, 0.0)
+            chosen[:size, C + half * LANES : C + (half + 1) * LANES] = jnp.sum(side, axis=1)
+        chosen[size:] = jnp.zeros((LANES - size, 2 * C), jnp.float32)
+
+    fewer = -1
+    for size in sizes:
+        pl.when((number > fewer) & (number <= size))(functools.partial(attend, size))
+        fewer = size
+
+    place = places[...].astype(jnp.bfloat16)
+    rest = chosen[...]
+    ordered = jnp.zeros((PADDED, 2 * C), jnp.float32)
+    for _ in range(3):
+        piece = rest.astype(jnp.bfloat16)
+        rest = rest - piece.astype(jnp.float32)
+        ordered = ordered + dot(place, piece)
+    here = jnp.sum(places[...], axis=1, keepdims=True) > 0.0
+    lane = iota((PADDED, LANES), 1)
     for half in range(2):
         into = slice(half * PADDED, (half + 1) * PADDED)
-        half_sums[into] = jnp.where(here, summed[:, half * LANES : (half + 1) * LANES], 0.0)
-        row = lax.rem(iota((PADDED, HEADS, LANES), 0) + half * PADDED, SHARE)
-        slot = lane - TILE * row
-        own = head - HALF * half
-        own = jnp.where((own >= 0) & (own < HALF), own, -TILE * LANES)
-        is_highest = slot == own
-        placed = jnp.where(is_highest, highest, 0.0) + jnp.where(slot == own + HALF, totals, 0.0)
-        absent = jnp.sum(jnp.where(is_highest, masked_low, 0.0), axis=1)
-        half_side[into] = jnp.where(here, jnp.sum(placed, axis=1), absent)
+        half_sums[into] = ordered[:, half * LANES : (half + 1) * LANES]
+        row = lax.rem(iota((PADDED, LANES), 0) + half * PADDED, SHARE)
+        side = ordered[:, C + half * LANES : C + (half + 1) * LANES]
+        absent = jnp.where(lane % TILE < HALF, masked_low, 0.0)
+        half_side[into] = jnp.where(lane // TILE == row, jnp.where(here, side, absent), 0.0)
 
     for buffer in (half_sums, half_side):
         buffer[HALVES:] = jnp.zeros((buffer.shape[0] - HALVES, LANES), jnp.float32)
@@ -211,7 +245,7 @@
     send_pixels.wait()
 
 
-def local(top, bottom, shifted, totals, weight, kv_weight, wide_queries, flags, shares):
+def local(top, bottom, shifted, totals, weight, kv_weight, wide_queries, places, shares):
     area = ROWS_IN * COLS_IN
     pixels = jax.ShapeDtypeStruct((2 * ROWS_IN, 2 * COLS_IN, C), jnp.bfloat16)
     vmem = pl.BlockSpec(memory_space=pltpu.VMEM)
@@ -226,13 +260,14 @@
             pltpu.VMEM((2, ROWS_IN, 2, 2 * COLS_IN, LANES), jnp.float32),
             pltpu.VMEM((4 * area, C), jnp.bfloat16),
             pltpu.VMEM((4 * area, C), jnp.bfloat16),
+            pltpu.VMEM((LANES, 2 * C), jnp.float32),
             pltpu.VMEM((HALVES + TILE, LANES), jnp.float32),
             pltpu.VMEM((HALVES + TILE, LANES), jnp.float32),
             pltpu.SemaphoreType.DMA,
         ],
         compiler_params=pltpu.CompilerParams(vmem_limit_bytes=40 << 20),
         cost_estimate=pl.CostEstimate(flops=2_000_000_000, bytes_accessed=4_000_000, transcendentals=800_000),
-    )(top, bottom, shifted, totals, weight, kv_weight, wide_queries, flags)
+    )(top, bottom, shifted, totals, weight, kv_weight, wide_queries, places)
 
 
 def widened(side, first):
@@ -321,12 +356,12 @@
         jnp.concatenate([part[at : at + 1] for part in (features, left, right)], axis=1) for at in (0, ROWS_IN - 1)
     ]
     top, bottom = swaps(first, last, "rows")
-    x, weight, kv_weight, wide_queries, flags = prepare(
+    x, weight, kv_weight, wide_queries, places = prepare(
         left, features, conv_weight, query_weight, kv_weight, queries, active_blocks
     )
     row_peers, col_peers = lax.axis_size("rows"), lax.axis_size("cols")
     shifted, totals = middle(x, left, right, weight)
-    pixels, part = local(top, bottom, shifted, totals, weight, kv_weight, wide_queries, flags, row_peers)
+    pixels, part = local(top, bottom, shifted, totals, weight, kv_weight, wide_queries, places, row_peers)
     parts = lax.all_to_all(part, "rows", 0, 0)
     copies = jax.ShapeDtypeStruct((col_peers, TILE, LANES), jnp.float32)
     parts = lax.all_to_all(on_device(merge_kernel, copies, parts), "cols", 0, 0)

time: 73.6 us -> 72.8 us (0.989)
  Pallas kernels: 6.76 us -> 5.95 us
    pallas_call x1, Pallas kernels: 2.82 us -> 2 us  [local(): pl.pallas_call(local_kernel, out_shape=(pixels, jax.ShapeDtypeStruct((sha...]
where the time goes in v5:
time: 72.8 us; the launch traced here: 72.3 us
  blocking collectives  48.9 us (67%)
  starting transfers between devices  14.8 us (20%)
  Pallas kernels  5.95 us (8%)
  other arithmetic  0.98 us (1%)
  between operations  0.78 us (1%)
  local copies, waits for them, and re-layouts  0.75 us (1%)
    all_to_all x1, blocking collectives, body(): parts = lax.all_to_all(part, 'rows', 0, 0)  20 us
    all_to_all x1, blocking collectives, body(): parts = lax.all_to_all(on_device(merge_kernel, copies, parts), 'cols', 0, 0)  16.9 us
    ppermute x4, starting transfers between devices, swaps(): lax.ppermute(edge, axis, pairs + [(j, i) for i, j in pairs])  14.8 us
    all_to_all x1, blocking collectives, body(): lax.all_to_all(on_device(attend_kernel, copies, parts), 'rows', 0, 0)  12 us
    pallas_call x1, Pallas kernels, local(): pl.pallas_call(local_kernel, out_shape=(pixels, jax.ShapeDtypeStruct((sha...  2 us
    pallas_call x1, Pallas kernels, prepare(): pl.pallas_call(prepare_kernel, out_shape=tuple((jax.ShapeDtypeStruct(t.sh...  1.87 us
    pallas_call x3, Pallas kernels, on_device(): pl.pallas_call(kernel, out_shape=out_shape, in_specs=[pl.BlockSpec(memory...  1.62 us
  transfers between devices with their start and end apart: 4, of which 1 were waited for; matrix products, arithmetic and copies ran while one was open for 1% of the time, Pallas kernels for 3%

profile of v5, /device:TPU:1, one launch (start us, length us, event | category | flops | bytes accessed | tf_op | source)
XLA Modules:
  0.0 72.3 jit_solution(3451697633886381542)
XLA Ops:
  0.6 0.9 %broadcast_select_fusion.1 = (bf16[16,1,256]{2,1,0:T(2,128)(2,1)S(1)}, bf16[16,1,256]{2,1,0:T(2,128)(2,1)S(1)}) fusion(pred[]{:T(512)S(6)} %eq.10, bf16[16,16,256]{2,1,0:T(8,128)(2,1)} %x_hbm.1), kind=kLoop, calls=%fused_computation.1 | loop fusion | flops 8192 | bytes 32769 | tf_op jit(solution)/shard_map/jit(_where)/select_n | solution.py:342
  1.6 4.6 %collective-permute-start = (bf16[16,1,256]{2,1,0:T(2,128)(2,1)S(1)}, bf16[16,1,256]{2,1,0:T(2,128)(2,1)S(1)}, u32[]{:S(2)}, u32[]{:S(2)}) collective-permute-start(bf16[16,1,256]{2,1,0:T(2,128)(2,1)S(1)} %get-tuple-element.27), channel_id=1, source_target_pairs={{1,2},{3,4},{5,6},{7,8},{9,10},{11,12},{13,14},{2,1},{4,3},{6,5},{... | collective-permute-start | bytes 24584 | tf_op jit(solution)/shard_map/ppermute | solution.py:344
  6.2 4.9 %collective-permute-start.1 = (bf16[16,1,256]{2,1,0:T(2,128)(2,1)S(1)}, bf16[16,1,256]{2,1,0:T(2,128)(2,1)S(1)}, u32[]{:S(2)}, u32[]{:S(2)}) collective-permute-start(bf16[16,1,256]{2,1,0:T(2,128)(2,1)S(1)} %get-tuple-element.28), channel_id=1, source_target_pairs={{0,1},{2,3},{4,5},{6,7},{8,9},{10,11},{12,13},{14,15},{1,0},{3,2},... | collective-permute-start | bytes 24584 | tf_op jit(solution)/shard_map/ppermute | solution.py:344
  11.0 0.7 %fusion = (bf16[1,16,256]{2,1,0:T(8,128)(2,1)S(1)}, bf16[1,16,256]{2,1,0:T(8,128)(2,1)S(1)}) fusion(bf16[16,16,256]{2,1,0:T(8,128)(2,1)} %x_hbm.1), kind=kLoop, calls=%fused_computation.10 | loop fusion | bytes 32768 | tf_op jit(solution)/shard_map/slice | solution.py:356
  11.8 0.0 collective-permute-done
  11.8 0.1 collective-permute-done.1
  11.9 0.7 collective-permute-start.3
  12.6 4.7 %collective-permute-start.2 = (bf16[1,18,256]{2,1,0:T(8,128)(2,1)S(1)}, bf16[1,18,256]{2,1,0:T(8,128)(2,1)S(1)}, u32[]{:S(2)}, u32[]{:S(2)}) collective-permute-start(bf16[1,18,256]{2,1,0:T(8,128)(2,1)S(1)} %get-tuple-element.34), channel_id=1, source_target_pairs={{0,16},{32,48},{64,80},{96,112},{128,144},{160,176},{192,208},{224... | collective-permute-start | bytes 27656 | tf_op jit(solution)/shard_map/ppermute | solution.py:344
  17.3 1.9 %shard_map.103 = (bf16[16,16,256]{2,1,0:T(8,128)(2,1)S(1)}, bf16[4,4,256,256]{3,2,1,0:T(8,128)(2,1)S(1)}, bf16[256,512]{1,0:T(8,128)(2,1)S(1)}, bf16[832,256]{1,0:T(8,128)(2,1)S(1)}, f32[104,128]{1,0:T(8,128)S(1)}) custom-call(bf16[16,1,256]{2,1,0:T(2,128)(2,1)S(1)} %get-tuple-element.29.after.left_ref, bf16[16,16,256]{2,1,0:T(8,128)(2,1)} %x_hbm.1, ...), custom_call_target="tpu_custom_call" | custom-call | flops 20000000 | bytes 6000000 | tf_op jit(solution)/shard_map/pallas_call | solution.py:100
  19.2 0.5 shard_map.104
  19.7 0.0 collective-permute-done.3
  19.7 0.0 collective-permute-done.2
  19.7 0.0 copy-start
  19.7 0.0 copy-start.1
  19.7 0.0 copy-start.2
  19.7 2.0 %shard_map.105 = (bf16[32,32,256]{2,1,0:T(8,128)(2,1)}, f32[32,8,128]{2,1,0:T(8,128)S(1)}) custom-call(bf16[1,18,256]{2,1,0:T(8,128)(2,1)S(1)} %get-tuple-element.32.top_ref, bf16[1,18,256]{2,1,0:T(8,128)(2,1)S(1)} %get-tuple-element.31.bottom_ref, bf16[3,256,256]{2,1,0:T(8,128)(2,1)S(1)} %get-tuple-element.16.shifted_ref, ...), custom_call_target="tpu_custom_call" | custom-call | flops 2000000000 | bytes 4000000 | tf_op jit(solution)/shard_map/pallas_call | solution.py:252
  21.8 20.0 %all_to_all.15.parts_ref = f32[32,8,128]{2,1,0:T(8,128)S(1)} all-to-all(f32[32,8,128]{2,1,0:T(8,128)S(1)} %get-tuple-element.22), channel_id=1, replica_groups=mesh['rows'=32,'cols'=16] {'rows'}, dimensions={0} | all-to-all | bytes 262144 | tf_op jit(solution)/shard_map/all_to_all | solution.py:365
  41.8 0.3 shard_map.106
  42.1 16.9 %all_to_all.16.parts_ref = f32[16,8,128]{2,1,0:T(8,128)S(1)} all-to-all(f32[16,8,128]{2,1,0:T(8,128)S(1)} %shard_map.106), channel_id=1, replica_groups=mesh['rows'=32,'cols'=16] {'cols'}, dimensions={0} | all-to-all | bytes 131072 | tf_op jit(solution)/shard_map/all_to_all | solution.py:367
  59.0 0.3 shard_map.107
  59.3 12.0 %all_to_all.17.attention_ref = bf16[32,8,128]{2,1,0:T(8,128)(2,1)S(1)} all-to-all(bf16[32,8,128]{2,1,0:T(8,128)(2,1)S(1)} %shard_map.107), channel_id=1, replica_groups=mesh['rows'=32,'cols'=16] {'rows'}, dimensions={0} | all-to-all | bytes 131072 | tf_op jit(solution)/shard_map/all_to_all | solution.py:369
  71.3 0.0 copy-done
  71.3 0.0 copy-done.1
  71.3 0.0 copy-done.2
  71.4 1.0 %shard_map.108 = (f32[100,256]{1,0:T(8,128)}, f32[100,256]{1,0:T(8,128)}) custom-call(bf16[32,8,128]{2,1,0:T(8,128)(2,1)S(1)} %all_to_all.17.attention_ref, bf16[256,256]{1,0:T(8,128)(2,1)S(1)} %copy-done.1, f32[100,256]{1,0:T(8,128)S(1)} %copy-done, f32[1,256]{1,0:T(1,128)S(1)} %bitcast.2), custom_call_target="tpu_custom_call" | custom-call | flops 10000000 | bytes 500000 | tf_op jit(solution)/shard_map/pallas_call | solution.py:327
  (4 shorter events, 0.1 us)
Async XLA Ops:
  1.6 10.2 %collective-permute-start = (bf16[16,1,256]{2,1,0:T(2,128)(2,1)S(1)}, bf16[16,1,256]{2,1,0:T(2,128)(2,1)S(1)}, u32[]{:S(2)}, u32[]{:S(2)}) collective-permute-start(bf16[16,1,256]{2,1,0:T(2,128)(2,1)S(1)} %get-tuple-element.27), channel_id=1, source_target_pairs={{1,2},{3,4},{5,6},{7,8},{9,10},{11,12},{13,14},{2,1},{4,3},{6,5},{... | collective-permute-start | bytes 24584 | tf_op jit(solution)/shard_map/ppermute | solution.py:344
  6.2 5.7 %collective-permute-start.1 = (bf16[16,1,256]{2,1,0:T(2,128)(2,1)S(1)}, bf16[16,1,256]{2,1,0:T(2,128)(2,1)S(1)}, u32[]{:S(2)}, u32[]{:S(2)}) collective-permute-start(bf16[16,1,256]{2,1,0:T(2,128)(2,1)S(1)} %get-tuple-element.28), channel_id=1, source_target_pairs={{0,1},{2,3},{4,5},{6,7},{8,9},{10,11},{12,13},{14,15},{1,0},{3,2},... | collective-permute-start | bytes 24584 | tf_op jit(solution)/shard_map/ppermute | solution.py:344
  11.9 7.8 %collective-permute-start.3 = (bf16[1,18,256]{2,1,0:T(8,128)(2,1)S(1)}, bf16[1,18,256]{2,1,0:T(8,128)(2,1)S(1)}, u32[]{:S(2)}, u32[]{:S(2)}) collective-permute-start(bf16[1,18,256]{2,1,0:T(8,128)(2,1)S(1)} %get-tuple-element.33), channel_id=1, source_target_pairs={{16,32},{48,64},{80,96},{112,128},{144,160},{176,192},{208,224},{2... | collective-permute-start | bytes 27656 | tf_op jit(solution)/shard_map/ppermute | solution.py:344
  12.6 7.1 %collective-permute-start.2 = (bf16[1,18,256]{2,1,0:T(8,128)(2,1)S(1)}, bf16[1,18,256]{2,1,0:T(8,128)(2,1)S(1)}, u32[]{:S(2)}, u32[]{:S(2)}) collective-permute-start(bf16[1,18,256]{2,1,0:T(8,128)(2,1)S(1)} %get-tuple-element.34), channel_id=1, source_target_pairs={{0,16},{32,48},{64,80},{96,112},{128,144},{160,176},{192,208},{224... | collective-permute-start | bytes 27656 | tf_op jit(solution)/shard_map/ppermute | solution.py:344
  19.7 51.6 %copy-start = (f32[100,256]{1,0:T(8,128)S(1)}, f32[100,256]{1,0:T(8,128)}, u32[]{:S(2)}) copy-start(f32[100,256]{1,0:T(8,128)} %queries_ref.1) | copy-start | bytes 307204
  19.7 51.6 %copy-start.1 = (bf16[256,256]{1,0:T(8,128)(2,1)S(1)}, bf16[256,256]{1,0:T(8,128)(2,1)}, u32[]{:S(2)}) copy-start(bf16[256,256]{1,0:T(8,128)(2,1)} %out_weight_ref.1) | copy-start | bytes 393220
  19.7 51.6 %copy-start.2 = (f32[256]{0:T(256)S(1)}, f32[256]{0:T(256)}, u32[]{:S(2)}) copy-start(f32[256]{0:T(256)} %param.14) | copy-start | bytes 3076

commit v6 on v5

--- a/solution.py
+++ b/solution.py
@@ -32,8 +32,19 @@
     return jnp.dot(a, b, preferred_element_type=jnp.float32)
 
 
+def pieces(x):
+    found = []
+    for _ in range(3):
+        found.append(x.astype(jnp.bfloat16))
+        x = x - found[-1].astype(jnp.float32)
+    return found
+
+
 def dot_exact(a, b):
-    return jnp.dot(a, b, preferred_element_type=jnp.float32, precision=lax.Precision.HIGHEST)
+    total = jnp.zeros((a.shape[0], b.shape[1]), jnp.float32)
+    for piece in pieces(a):
+        total = total + dot(piece, b.astype(jnp.bfloat16))
+    return total
 
 
 def iota(shape, dim):
@@ -217,11 +228,8 @@
         fewer = size
 
     place = places[...].astype(jnp.bfloat16)
-    rest = chosen[...]
     ordered = jnp.zeros((PADDED, 2 * C), jnp.float32)
-    for _ in range(3):
-        piece = rest.astype(jnp.bfloat16)
-        rest = rest - piece.astype(jnp.float32)
+    for piece in pieces(chosen[...]):
         ordered = ordered + dot(place, piece)
     here = jnp.sum(places[...], axis=1, keepdims=True) > 0.0
     lane = iota((PADDED, LANES), 1)

time: 72.8 us -> 72.6 us (level)
  no operation moved by 1% of the time
where the time goes in v6:
time: 72.6 us; the launch traced here: 72.2 us
  blocking collectives  48.8 us (67%)
  starting transfers between devices  14.8 us (20%)
  Pallas kernels  5.97 us (8%)
  other arithmetic  0.98 us (1%)
  between operations  0.78 us (1%)
  local copies, waits for them, and re-layouts  0.75 us (1%)
    all_to_all x1, blocking collectives, body(): parts = lax.all_to_all(part, 'rows', 0, 0)  19.8 us
    all_to_all x1, blocking collectives, body(): parts = lax.all_to_all(on_device(merge_kernel, copies, parts), 'cols', 0, 0)  16.9 us
    ppermute x4, starting transfers between devices, swaps(): lax.ppermute(edge, axis, pairs + [(j, i) for i, j in pairs])  14.8 us
    all_to_all x1, blocking collectives, body(): lax.all_to_all(on_device(attend_kernel, copies, parts), 'rows', 0, 0)  12.1 us
    pallas_call x1, Pallas kernels, local(): pl.pallas_call(local_kernel, out_shape=(pixels, jax.ShapeDtypeStruct((sha...  2.17 us
    pallas_call x1, Pallas kernels, prepare(): pl.pallas_call(prepare_kernel, out_shape=tuple((jax.ShapeDtypeStruct(t.sh...  1.87 us
    pallas_call x3, Pallas kernels, on_device(): pl.pallas_call(kernel, out_shape=out_shape, in_specs=[pl.BlockSpec(memory...  1.48 us
  transfers between devices with their start and end apart: 4, of which 1 were waited for; matrix products, arithmetic and copies ran while one was open for 1% of the time, Pallas kernels for 3%

profile of v6, /device:TPU:1, one launch (start us, length us, event | category | flops | bytes accessed | tf_op | source)
XLA Modules:
  0.0 72.2 jit_solution(618670338304476532)
XLA Ops:
  0.6 0.9 %broadcast_select_fusion.1 = (bf16[16,1,256]{2,1,0:T(2,128)(2,1)S(1)}, bf16[16,1,256]{2,1,0:T(2,128)(2,1)S(1)}) fusion(pred[]{:T(512)S(6)} %eq.10, bf16[16,16,256]{2,1,0:T(8,128)(2,1)} %x_hbm.1), kind=kLoop, calls=%fused_computation.1 | loop fusion | flops 8192 | bytes 32769 | tf_op jit(solution)/shard_map/jit(_where)/select_n | solution.py:350
  1.6 4.6 %collective-permute-start = (bf16[16,1,256]{2,1,0:T(2,128)(2,1)S(1)}, bf16[16,1,256]{2,1,0:T(2,128)(2,1)S(1)}, u32[]{:S(2)}, u32[]{:S(2)}) collective-permute-start(bf16[16,1,256]{2,1,0:T(2,128)(2,1)S(1)} %get-tuple-element.27), channel_id=1, source_target_pairs={{1,2},{3,4},{5,6},{7,8},{9,10},{11,12},{13,14},{2,1},{4,3},{6,5},{... | collective-permute-start | bytes 24584 | tf_op jit(solution)/shard_map/ppermute | solution.py:352
  6.2 4.9 %collective-permute-start.1 = (bf16[16,1,256]{2,1,0:T(2,128)(2,1)S(1)}, bf16[16,1,256]{2,1,0:T(2,128)(2,1)S(1)}, u32[]{:S(2)}, u32[]{:S(2)}) collective-permute-start(bf16[16,1,256]{2,1,0:T(2,128)(2,1)S(1)} %get-tuple-element.28), channel_id=1, source_target_pairs={{0,1},{2,3},{4,5},{6,7},{8,9},{10,11},{12,13},{14,15},{1,0},{3,2},... | collective-permute-start | bytes 24584 | tf_op jit(solution)/shard_map/ppermute | solution.py:352
  11.0 0.7 %fusion = (bf16[1,16,256]{2,1,0:T(8,128)(2,1)S(1)}, bf16[1,16,256]{2,1,0:T(8,128)(2,1)S(1)}) fusion(bf16[16,16,256]{2,1,0:T(8,128)(2,1)} %x_hbm.1), kind=kLoop, calls=%fused_computation.10 | loop fusion | bytes 32768 | tf_op jit(solution)/shard_map/slice | solution.py:364
  11.8 0.0 collective-permute-done
  11.8 0.1 collective-permute-done.1
  11.9 0.7 collective-permute-start.3
  12.6 4.7 %collective-permute-start.2 = (bf16[1,18,256]{2,1,0:T(8,128)(2,1)S(1)}, bf16[1,18,256]{2,1,0:T(8,128)(2,1)S(1)}, u32[]{:S(2)}, u32[]{:S(2)}) collective-permute-start(bf16[1,18,256]{2,1,0:T(8,128)(2,1)S(1)} %get-tuple-element.34), channel_id=1, source_target_pairs={{0,16},{32,48},{64,80},{96,112},{128,144},{160,176},{192,208},{224... | collective-permute-start | bytes 27656 | tf_op jit(solution)/shard_map/ppermute | solution.py:352
  17.3 1.9 %shard_map.103 = (bf16[16,16,256]{2,1,0:T(8,128)(2,1)S(1)}, bf16[4,4,256,256]{3,2,1,0:T(8,128)(2,1)S(1)}, bf16[256,512]{1,0:T(8,128)(2,1)S(1)}, bf16[832,256]{1,0:T(8,128)(2,1)S(1)}, f32[104,128]{1,0:T(8,128)S(1)}) custom-call(bf16[16,1,256]{2,1,0:T(2,128)(2,1)S(1)} %get-tuple-element.29.after.left_ref, bf16[16,16,256]{2,1,0:T(8,128)(2,1)} %x_hbm.1, ...), custom_call_target="tpu_custom_call" | custom-call | flops 20000000 | bytes 6000000 | tf_op jit(solution)/shard_map/pallas_call | solution.py:111
  19.2 0.5 shard_map.104
  19.7 0.0 collective-permute-done.3
  19.7 0.0 collective-permute-done.2
  19.7 0.0 copy-start
  19.7 0.0 copy-start.1
  19.7 0.0 copy-start.2
  19.7 2.2 %shard_map.105 = (bf16[32,32,256]{2,1,0:T(8,128)(2,1)}, f32[32,8,128]{2,1,0:T(8,128)S(1)}) custom-call(bf16[1,18,256]{2,1,0:T(8,128)(2,1)S(1)} %get-tuple-element.32.top_ref, bf16[1,18,256]{2,1,0:T(8,128)(2,1)S(1)} %get-tuple-element.31.bottom_ref, bf16[3,256,256]{2,1,0:T(8,128)(2,1)S(1)} %get-tuple-element.16.shifted_ref, ...), custom_call_target="tpu_custom_call" | custom-call | flops 2000000000 | bytes 4000000 | tf_op jit(solution)/shard_map/pallas_call | solution.py:260
  21.9 19.8 %all_to_all.15.parts_ref = f32[32,8,128]{2,1,0:T(8,128)S(1)} all-to-all(f32[32,8,128]{2,1,0:T(8,128)S(1)} %get-tuple-element.22), channel_id=1, replica_groups=mesh['rows'=32,'cols'=16] {'rows'}, dimensions={0} | all-to-all | bytes 262144 | tf_op jit(solution)/shard_map/all_to_all | solution.py:373
  41.8 0.2 shard_map.106
  42.0 16.9 %all_to_all.16.parts_ref = f32[16,8,128]{2,1,0:T(8,128)S(1)} all-to-all(f32[16,8,128]{2,1,0:T(8,128)S(1)} %shard_map.106), channel_id=1, replica_groups=mesh['rows'=32,'cols'=16] {'cols'}, dimensions={0} | all-to-all | bytes 131072 | tf_op jit(solution)/shard_map/all_to_all | solution.py:375
  58.9 0.3 shard_map.107
  59.1 12.1 %all_to_all.17.attention_ref = bf16[32,8,128]{2,1,0:T(8,128)(2,1)S(1)} all-to-all(bf16[32,8,128]{2,1,0:T(8,128)(2,1)S(1)} %shard_map.107), channel_id=1, replica_groups=mesh['rows'=32,'cols'=16] {'rows'}, dimensions={0} | all-to-all | bytes 131072 | tf_op jit(solution)/shard_map/all_to_all | solution.py:377
  71.2 0.0 copy-done
  71.2 0.0 copy-done.1
  71.2 0.0 copy-done.2
  71.2 1.0 %shard_map.108 = (f32[100,256]{1,0:T(8,128)}, f32[100,256]{1,0:T(8,128)}) custom-call(bf16[32,8,128]{2,1,0:T(8,128)(2,1)S(1)} %all_to_all.17.attention_ref, bf16[256,256]{1,0:T(8,128)(2,1)S(1)} %copy-done.1, f32[100,256]{1,0:T(8,128)S(1)} %copy-done, f32[1,256]{1,0:T(1,128)S(1)} %bitcast.2), custom_call_target="tpu_custom_call" | custom-call | flops 10000000 | bytes 500000 | tf_op jit(solution)/shard_map/pallas_call | solution.py:335
  (4 shorter events, 0.1 us)
Async XLA Ops:
  1.6 10.2 %collective-permute-start = (bf16[16,1,256]{2,1,0:T(2,128)(2,1)S(1)}, bf16[16,1,256]{2,1,0:T(2,128)(2,1)S(1)}, u32[]{:S(2)}, u32[]{:S(2)}) collective-permute-start(bf16[16,1,256]{2,1,0:T(2,128)(2,1)S(1)} %get-tuple-element.27), channel_id=1, source_target_pairs={{1,2},{3,4},{5,6},{7,8},{9,10},{11,12},{13,14},{2,1},{4,3},{6,5},{... | collective-permute-start | bytes 24584 | tf_op jit(solution)/shard_map/ppermute | solution.py:352
  6.2 5.7 %collective-permute-start.1 = (bf16[16,1,256]{2,1,0:T(2,128)(2,1)S(1)}, bf16[16,1,256]{2,1,0:T(2,128)(2,1)S(1)}, u32[]{:S(2)}, u32[]{:S(2)}) collective-permute-start(bf16[16,1,256]{2,1,0:T(2,128)(2,1)S(1)} %get-tuple-element.28), channel_id=1, source_target_pairs={{0,1},{2,3},{4,5},{6,7},{8,9},{10,11},{12,13},{14,15},{1,0},{3,2},... | collective-permute-start | bytes 24584 | tf_op jit(solution)/shard_map/ppermute | solution.py:352
  11.9 7.8 %collective-permute-start.3 = (bf16[1,18,256]{2,1,0:T(8,128)(2,1)S(1)}, bf16[1,18,256]{2,1,0:T(8,128)(2,1)S(1)}, u32[]{:S(2)}, u32[]{:S(2)}) collective-permute-start(bf16[1,18,256]{2,1,0:T(8,128)(2,1)S(1)} %get-tuple-element.33), channel_id=1, source_target_pairs={{16,32},{48,64},{80,96},{112,128},{144,160},{176,192},{208,224},{2... | collective-permute-start | bytes 27656 | tf_op jit(solution)/shard_map/ppermute | solution.py:352
  12.6 7.1 %collective-permute-start.2 = (bf16[1,18,256]{2,1,0:T(8,128)(2,1)S(1)}, bf16[1,18,256]{2,1,0:T(8,128)(2,1)S(1)}, u32[]{:S(2)}, u32[]{:S(2)}) collective-permute-start(bf16[1,18,256]{2,1,0:T(8,128)(2,1)S(1)} %get-tuple-element.34), channel_id=1, source_target_pairs={{0,16},{32,48},{64,80},{96,112},{128,144},{160,176},{192,208},{224... | collective-permute-start | bytes 27656 | tf_op jit(solution)/shard_map/ppermute | solution.py:352
  19.7 51.5 %copy-start = (f32[100,256]{1,0:T(8,128)S(1)}, f32[100,256]{1,0:T(8,128)}, u32[]{:S(2)}) copy-start(f32[100,256]{1,0:T(8,128)} %queries_ref.1) | copy-start | bytes 307204
  19.7 51.5 %copy-start.1 = (bf16[256,256]{1,0:T(8,128)(2,1)S(1)}, bf16[256,256]{1,0:T(8,128)(2,1)}, u32[]{:S(2)}) copy-start(bf16[256,256]{1,0:T(8,128)(2,1)} %out_weight_ref.1) | copy-start | bytes 393220
  19.7 51.5 %copy-start.2 = (f32[256]{0:T(256)S(1)}, f32[256]{0:T(256)}, u32[]{:S(2)}) copy-start(f32[256]{0:T(256)} %param.14) | copy-start | bytes 3076

commit v7 on v6

--- a/solution.py
+++ b/solution.py
@@ -129,8 +129,8 @@
     shifted[1] = x_ref[...].reshape(area, C)
     x = x_ref[...].astype(jnp.float32)
     column = iota((ROWS_IN, COLS_IN, C), 1)
-    left = left_ref[...].astype(jnp.float32)
-    right = right_ref[...].astype(jnp.float32)
+    left = left_ref[...].astype(jnp.float32)[:, None, :]
+    right = right_ref[...].astype(jnp.float32)[:, None, :]
     before = jnp.where(column == 0, left, pltpu.roll(x, 1, 1))
     after = jnp.where(column == COLS_IN - 1, right, pltpu.roll(x, COLS_IN - 1, 1))
     shifted[0] = before.astype(jnp.bfloat16).reshape(area, C)
@@ -359,9 +359,9 @@
 def body(
     features, conv_weight, query_weight, kv_weight, out_weight, queries, norm_gain, active_blocks
 ):
-    left, right = swaps(features[:, :1], features[:, -1:], "cols")
+    left, right = swaps(features[:, 0], features[:, -1], "cols")
     first, last = [
-        jnp.concatenate([part[at : at + 1] for part in (features, left, right)], axis=1) for at in (0, ROWS_IN - 1)
+        jnp.concatenate([features[at], left[at : at + 1], right[at : at + 1]])[None] for at in (0, ROWS_IN - 1)
     ]
     top, bottom = swaps(first, last, "rows")
     x, weight, kv_weight, wide_queries, places = prepare(

time: 72.6 us -> 72.5 us (level)
  other arithmetic: 0.98 us -> 0.04 us
  local copies, waits for them, and re-layouts: 0.75 us -> 1.66 us
    select_n x2, other arithmetic: 0.93 us -> 0.02 us  [swaps(): jnp.where(odd, last, first)]
    slice x2, local copies, waits for them, and re-layouts: 0.73 us -> 1.63 us  [the longest x1 0.9 us: body(): left, right = swaps(features[:, 0], features[:, -1], 'cols')]
where the time goes in v7:
time: 72.5 us; the launch traced here: 72.1 us
  blocking collectives  48.9 us (67%)
  starting transfers between devices  14.8 us (20%)
  Pallas kernels  5.8 us (8%)
  local copies, waits for them, and re-layouts  1.66 us (2%)
  between operations  0.77 us (1%)
    all_to_all x1, blocking collectives, body(): parts = lax.all_to_all(part, 'rows', 0, 0)  20 us
    all_to_all x1, blocking collectives, body(): parts = lax.all_to_all(on_device(merge_kernel, copies, parts), 'cols', 0, 0)  16.9 us
    ppermute x4, starting transfers between devices, swaps(): lax.ppermute(edge, axis, pairs + [(j, i) for i, j in pairs])  14.8 us
    all_to_all x1, blocking collectives, body(): lax.all_to_all(on_device(attend_kernel, copies, parts), 'rows', 0, 0)  12 us
    pallas_call x1, Pallas kernels, local(): pl.pallas_call(local_kernel, out_shape=(pixels, jax.ShapeDtypeStruct((sha...  2 us
    pallas_call x1, Pallas kernels, prepare(): pl.pallas_call(prepare_kernel, out_shape=tuple((jax.ShapeDtypeStruct(t.sh...  1.87 us
    pallas_call x3, Pallas kernels, on_device(): pl.pallas_call(kernel, out_shape=out_shape, in_specs=[pl.BlockSpec(memory...  1.48 us
  transfers between devices with their start and end apart: 4, of which 1 were waited for; matrix products, arithmetic and copies ran while one was open for 1% of the time, Pallas kernels for 3%

profile of v7, /device:TPU:1, one launch (start us, length us, event | category | flops | bytes accessed | tf_op | source)
XLA Modules:
  0.0 72.1 jit_solution(8910449524069069886)
XLA Ops:
  0.6 0.9 %fusion.1 = (bf16[16,1,256]{2,1,0:T(2,128)(2,1)S(1)}, bf16[16,1,256]{2,1,0:T(2,128)(2,1)S(1)}) fusion(bf16[16,16,256]{2,1,0:T(8,128)(2,1)} %x_hbm.1), kind=kLoop, calls=%fused_computation.15 | loop fusion | bytes 32768 | tf_op jit(solution)/shard_map/slice | solution.py:362
  1.6 4.6 %collective-permute-start = (bf16[16,256]{1,0:T(8,128)(2,1)S(1)}, bf16[16,256]{1,0:T(8,128)(2,1)S(1)}, u32[]{:S(2)}, u32[]{:S(2)}) collective-permute-start(bf16[16,256]{1,0:T(8,128)(2,1)S(1)} %get-tuple-element.29), channel_id=1, source_target_pairs={{1,2},{3,4},{5,6},{7,8},{9,10},{11,12},{13,14},{2,1},{4,3},{6,5},{... | collective-permute-start | bytes 24584 | tf_op jit(solution)/shard_map/ppermute | solution.py:352
  6.2 4.9 %collective-permute-start.1 = (bf16[16,256]{1,0:T(8,128)(2,1)S(1)}, bf16[16,256]{1,0:T(8,128)(2,1)S(1)}, u32[]{:S(2)}, u32[]{:S(2)}) collective-permute-start(bf16[16,256]{1,0:T(8,128)(2,1)S(1)} %get-tuple-element.30), channel_id=1, source_target_pairs={{0,1},{2,3},{4,5},{6,7},{8,9},{10,11},{12,13},{14,15},{1,0},{3,2},... | collective-permute-start | bytes 24584 | tf_op jit(solution)/shard_map/ppermute | solution.py:352
  11.0 0.7 %fusion = (bf16[1,16,256]{2,1,0:T(8,128)(2,1)S(1)}, bf16[1,16,256]{2,1,0:T(8,128)(2,1)S(1)}) fusion(bf16[16,16,256]{2,1,0:T(8,128)(2,1)} %x_hbm.1), kind=kLoop, calls=%fused_computation.14 | loop fusion | bytes 32768 | tf_op jit(solution)/shard_map/slice | solution.py:364
  11.8 0.0 collective-permute-done
  11.8 0.1 collective-permute-done.1
  11.9 0.7 collective-permute-start.3
  12.5 4.7 %collective-permute-start.2 = (bf16[1,18,256]{2,1,0:T(8,128)(2,1)S(1)}, bf16[1,18,256]{2,1,0:T(8,128)(2,1)S(1)}, u32[]{:S(2)}, u32[]{:S(2)}) collective-permute-start(bf16[1,18,256]{2,1,0:T(8,128)(2,1)S(1)} %get-tuple-element.34), channel_id=1, source_target_pairs={{0,16},{32,48},{64,80},{96,112},{128,144},{160,176},{192,208},{224... | collective-permute-start | bytes 27656 | tf_op jit(solution)/shard_map/ppermute | solution.py:352
  17.3 1.9 %shard_map.103 = (bf16[16,16,256]{2,1,0:T(8,128)(2,1)S(1)}, bf16[4,4,256,256]{3,2,1,0:T(8,128)(2,1)S(1)}, bf16[256,512]{1,0:T(8,128)(2,1)S(1)}, bf16[832,256]{1,0:T(8,128)(2,1)S(1)}, f32[104,128]{1,0:T(8,128)S(1)}) custom-call(bf16[16,256]{1,0:T(8,128)(2,1)S(1)} %get-tuple-element.35.after.left_ref, bf16[16,16,256]{2,1,0:T(8,128)(2,1)} %x_hbm.1, ...), custom_call_target="tpu_custom_call" | custom-call | flops 20000000 | bytes 6000000 | tf_op jit(solution)/shard_map/pallas_call | solution.py:111
  19.2 0.5 shard_map.104
  19.6 0.0 collective-permute-done.3
  19.6 0.0 collective-permute-done.2
  19.7 0.0 copy-start
  19.7 0.0 copy-start.1
  19.7 0.0 copy-start.2
  19.7 2.0 %shard_map.105 = (bf16[32,32,256]{2,1,0:T(8,128)(2,1)}, f32[32,8,128]{2,1,0:T(8,128)S(1)}) custom-call(bf16[1,18,256]{2,1,0:T(8,128)(2,1)S(1)} %get-tuple-element.32.top_ref, bf16[1,18,256]{2,1,0:T(8,128)(2,1)S(1)} %get-tuple-element.31.bottom_ref, bf16[3,256,256]{2,1,0:T(8,128)(2,1)S(1)} %get-tuple-element.16.shifted_ref, ...), custom_call_target="tpu_custom_call" | custom-call | flops 2000000000 | bytes 4000000 | tf_op jit(solution)/shard_map/pallas_call | solution.py:260
  21.7 20.0 %all_to_all.15.parts_ref = f32[32,8,128]{2,1,0:T(8,128)S(1)} all-to-all(f32[32,8,128]{2,1,0:T(8,128)S(1)} %get-tuple-element.22), channel_id=1, replica_groups=mesh['rows'=32,'cols'=16] {'rows'}, dimensions={0} | all-to-all | bytes 262144 | tf_op jit(solution)/shard_map/all_to_all | solution.py:373
  41.7 0.2 shard_map.106
  42.0 16.9 %all_to_all.16.parts_ref = f32[16,8,128]{2,1,0:T(8,128)S(1)} all-to-all(f32[16,8,128]{2,1,0:T(8,128)S(1)} %shard_map.106), channel_id=1, replica_groups=mesh['rows'=32,'cols'=16] {'cols'}, dimensions={0} | all-to-all | bytes 131072 | tf_op jit(solution)/shard_map/all_to_all | solution.py:375
  58.8 0.3 shard_map.107
  59.1 12.0 %all_to_all.17.attention_ref = bf16[32,8,128]{2,1,0:T(8,128)(2,1)S(1)} all-to-all(bf16[32,8,128]{2,1,0:T(8,128)(2,1)S(1)} %shard_map.107), channel_id=1, replica_groups=mesh['rows'=32,'cols'=16] {'rows'}, dimensions={0} | all-to-all | bytes 131072 | tf_op jit(solution)/shard_map/all_to_all | solution.py:377
  71.1 0.0 copy-done
  71.1 0.0 copy-done.1
  71.1 0.0 copy-done.2
  71.1 1.0 %shard_map.108 = (f32[100,256]{1,0:T(8,128)}, f32[100,256]{1,0:T(8,128)}) custom-call(bf16[32,8,128]{2,1,0:T(8,128)(2,1)S(1)} %all_to_all.17.attention_ref, bf16[256,256]{1,0:T(8,128)(2,1)S(1)} %copy-done.1, f32[100,256]{1,0:T(8,128)S(1)} %copy-done, f32[1,256]{1,0:T(1,128)S(1)} %bitcast.14), custom_call_target="tpu_custom_call" | custom-call | flops 10000000 | bytes 500000 | tf_op jit(solution)/shard_map/pallas_call | solution.py:335
  (5 shorter events, 0.0 us)
Async XLA Ops:
  1.6 10.2 %collective-permute-start = (bf16[16,256]{1,0:T(8,128)(2,1)S(1)}, bf16[16,256]{1,0:T(8,128)(2,1)S(1)}, u32[]{:S(2)}, u32[]{:S(2)}) collective-permute-start(bf16[16,256]{1,0:T(8,128)(2,1)S(1)} %get-tuple-element.29), channel_id=1, source_target_pairs={{1,2},{3,4},{5,6},{7,8},{9,10},{11,12},{13,14},{2,1},{4,3},{6,5},{... | collective-permute-start | bytes 24584 | tf_op jit(solution)/shard_map/ppermute | solution.py:352
  6.2 5.7 %collective-permute-start.1 = (bf16[16,256]{1,0:T(8,128)(2,1)S(1)}, bf16[16,256]{1,0:T(8,128)(2,1)S(1)}, u32[]{:S(2)}, u32[]{:S(2)}) collective-permute-start(bf16[16,256]{1,0:T(8,128)(2,1)S(1)} %get-tuple-element.30), channel_id=1, source_target_pairs={{0,1},{2,3},{4,5},{6,7},{8,9},{10,11},{12,13},{14,15},{1,0},{3,2},... | collective-permute-start | bytes 24584 | tf_op jit(solution)/shard_map/ppermute | solution.py:352
  11.9 7.8 %collective-permute-start.3 = (bf16[1,18,256]{2,1,0:T(8,128)(2,1)S(1)}, bf16[1,18,256]{2,1,0:T(8,128)(2,1)S(1)}, u32[]{:S(2)}, u32[]{:S(2)}) collective-permute-start(bf16[1,18,256]{2,1,0:T(8,128)(2,1)S(1)} %get-tuple-element.33), channel_id=1, source_target_pairs={{16,32},{48,64},{80,96},{112,128},{144,160},{176,192},{208,224},{2... | collective-permute-start | bytes 27656 | tf_op jit(solution)/shard_map/ppermute | solution.py:352
  12.5 7.1 %collective-permute-start.2 = (bf16[1,18,256]{2,1,0:T(8,128)(2,1)S(1)}, bf16[1,18,256]{2,1,0:T(8,128)(2,1)S(1)}, u32[]{:S(2)}, u32[]{:S(2)}) collective-permute-start(bf16[1,18,256]{2,1,0:T(8,128)(2,1)S(1)} %get-tuple-element.34), channel_id=1, source_target_pairs={{0,16},{32,48},{64,80},{96,112},{128,144},{160,176},{192,208},{224... | collective-permute-start | bytes 27656 | tf_op jit(solution)/shard_map/ppermute | solution.py:352
  19.7 51.4 %copy-start = (f32[100,256]{1,0:T(8,128)S(1)}, f32[100,256]{1,0:T(8,128)}, u32[]{:S(2)}) copy-start(f32[100,256]{1,0:T(8,128)} %queries_ref.1) | copy-start | bytes 307204
  19.7 51.4 %copy-start.1 = (bf16[256,256]{1,0:T(8,128)(2,1)S(1)}, bf16[256,256]{1,0:T(8,128)(2,1)}, u32[]{:S(2)}) copy-start(bf16[256,256]{1,0:T(8,128)(2,1)} %out_weight_ref.1) | copy-start | bytes 393220
  19.7 51.4 %copy-start.2 = (f32[256]{0:T(256)S(1)}, f32[256]{0:T(256)}, u32[]{:S(2)}) copy-start(f32[256]{0:T(256)} %param.14) | copy-start | bytes 3076

commit v8 on v7

--- a/solution.py
+++ b/solution.py
@@ -22,7 +22,7 @@
 TILE = 8
 HALVES = 2 * PADDED
 
-sizes = (16, 32, 48, PADDED)
+sizes = (8, 16, 24, 32, 48, PADDED)
 
 masked_low = -1e30
 tap_table = (((1, 1), (0, 3)), ((1, 2), (2, 0)))

time: 72.5 us -> 72.6 us (level)
  no operation moved by 1% of the time
where the time goes in v8:
time: 72.6 us; the launch traced here: 72.5 us
  blocking collectives  49.3 us (68%)
  starting transfers between devices  14.8 us (20%)
  Pallas kernels  5.72 us (8%)
  local copies, waits for them, and re-layouts  1.66 us (2%)
  between operations  0.77 us (1%)
    all_to_all x1, blocking collectives, body(): parts = lax.all_to_all(part, 'rows', 0, 0)  20 us
    all_to_all x1, blocking collectives, body(): parts = lax.all_to_all(on_device(merge_kernel, copies, parts), 'cols', 0, 0)  17.3 us
    ppermute x4, starting transfers between devices, swaps(): lax.ppermute(edge, axis, pairs + [(j, i) for i, j in pairs])  14.8 us
    all_to_all x1, blocking collectives, body(): lax.all_to_all(on_device(attend_kernel, copies, parts), 'rows', 0, 0)  12.1 us
    pallas_call x1, Pallas kernels, local(): pl.pallas_call(local_kernel, out_shape=(pixels, jax.ShapeDtypeStruct((sha...  1.91 us
    pallas_call x1, Pallas kernels, prepare(): pl.pallas_call(prepare_kernel, out_shape=tuple((jax.ShapeDtypeStruct(t.sh...  1.87 us
    pallas_call x3, Pallas kernels, on_device(): pl.pallas_call(kernel, out_shape=out_shape, in_specs=[pl.BlockSpec(memory...  1.48 us
  transfers between devices with their start and end apart: 4, of which 1 were waited for; matrix products, arithmetic and copies ran while one was open for 1% of the time, Pallas kernels for 3%

profile of v8, /device:TPU:1, one launch (start us, length us, event | category | flops | bytes accessed | tf_op | source)
XLA Modules:
  0.0 72.5 jit_solution(14819800684991446657)
XLA Ops:
  0.6 0.9 %fusion.1 = (bf16[16,1,256]{2,1,0:T(2,128)(2,1)S(1)}, bf16[16,1,256]{2,1,0:T(2,128)(2,1)S(1)}) fusion(bf16[16,16,256]{2,1,0:T(8,128)(2,1)} %x_hbm.1), kind=kLoop, calls=%fused_computation.15 | loop fusion | bytes 32768 | tf_op jit(solution)/shard_map/slice | solution.py:362
  1.6 4.6 %collective-permute-start = (bf16[16,256]{1,0:T(8,128)(2,1)S(1)}, bf16[16,256]{1,0:T(8,128)(2,1)S(1)}, u32[]{:S(2)}, u32[]{:S(2)}) collective-permute-start(bf16[16,256]{1,0:T(8,128)(2,1)S(1)} %get-tuple-element.29), channel_id=1, source_target_pairs={{1,2},{3,4},{5,6},{7,8},{9,10},{11,12},{13,14},{2,1},{4,3},{6,5},{... | collective-permute-start | bytes 24584 | tf_op jit(solution)/shard_map/ppermute | solution.py:352
  6.2 4.9 %collective-permute-start.1 = (bf16[16,256]{1,0:T(8,128)(2,1)S(1)}, bf16[16,256]{1,0:T(8,128)(2,1)S(1)}, u32[]{:S(2)}, u32[]{:S(2)}) collective-permute-start(bf16[16,256]{1,0:T(8,128)(2,1)S(1)} %get-tuple-element.30), channel_id=1, source_target_pairs={{0,1},{2,3},{4,5},{6,7},{8,9},{10,11},{12,13},{14,15},{1,0},{3,2},... | collective-permute-start | bytes 24584 | tf_op jit(solution)/shard_map/ppermute | solution.py:352
  11.0 0.7 %fusion = (bf16[1,16,256]{2,1,0:T(8,128)(2,1)S(1)}, bf16[1,16,256]{2,1,0:T(8,128)(2,1)S(1)}) fusion(bf16[16,16,256]{2,1,0:T(8,128)(2,1)} %x_hbm.1), kind=kLoop, calls=%fused_computation.14 | loop fusion | bytes 32768 | tf_op jit(solution)/shard_map/slice | solution.py:364
  11.8 0.0 collective-permute-done
  11.8 0.1 collective-permute-done.1
  11.9 0.7 collective-permute-start.3
  12.5 4.7 %collective-permute-start.2 = (bf16[1,18,256]{2,1,0:T(8,128)(2,1)S(1)}, bf16[1,18,256]{2,1,0:T(8,128)(2,1)S(1)}, u32[]{:S(2)}, u32[]{:S(2)}) collective-permute-start(bf16[1,18,256]{2,1,0:T(8,128)(2,1)S(1)} %get-tuple-element.34), channel_id=1, source_target_pairs={{0,16},{32,48},{64,80},{96,112},{128,144},{160,176},{192,208},{224... | collective-permute-start | bytes 27656 | tf_op jit(solution)/shard_map/ppermute | solution.py:352
  17.3 1.9 %shard_map.103 = (bf16[16,16,256]{2,1,0:T(8,128)(2,1)S(1)}, bf16[4,4,256,256]{3,2,1,0:T(8,128)(2,1)S(1)}, bf16[256,512]{1,0:T(8,128)(2,1)S(1)}, bf16[832,256]{1,0:T(8,128)(2,1)S(1)}, f32[104,128]{1,0:T(8,128)S(1)}) custom-call(bf16[16,256]{1,0:T(8,128)(2,1)S(1)} %get-tuple-element.35.after.left_ref, bf16[16,16,256]{2,1,0:T(8,128)(2,1)} %x_hbm.1, ...), custom_call_target="tpu_custom_call" | custom-call | flops 20000000 | bytes 6000000 | tf_op jit(solution)/shard_map/pallas_call | solution.py:111
  19.2 0.5 shard_map.104
  19.6 0.0 collective-permute-done.3
  19.6 0.0 collective-permute-done.2
  19.7 0.0 copy-start
  19.7 0.0 copy-start.1
  19.7 0.0 copy-start.2
  19.7 1.9 %shard_map.105 = (bf16[32,32,256]{2,1,0:T(8,128)(2,1)}, f32[32,8,128]{2,1,0:T(8,128)S(1)}) custom-call(bf16[1,18,256]{2,1,0:T(8,128)(2,1)S(1)} %get-tuple-element.32.top_ref, bf16[1,18,256]{2,1,0:T(8,128)(2,1)S(1)} %get-tuple-element.31.bottom_ref, bf16[3,256,256]{2,1,0:T(8,128)(2,1)S(1)} %get-tuple-element.16.shifted_ref, ...), custom_call_target="tpu_custom_call" | custom-call | flops 2000000000 | bytes 4000000 | tf_op jit(solution)/shard_map/pallas_call | solution.py:260
  21.6 20.0 %all_to_all.15.parts_ref = f32[32,8,128]{2,1,0:T(8,128)S(1)} all-to-all(f32[32,8,128]{2,1,0:T(8,128)S(1)} %get-tuple-element.22), channel_id=1, replica_groups=mesh['rows'=32,'cols'=16] {'rows'}, dimensions={0} | all-to-all | bytes 262144 | tf_op jit(solution)/shard_map/all_to_all | solution.py:373
  41.6 0.2 shard_map.106
  41.9 17.3 %all_to_all.16.parts_ref = f32[16,8,128]{2,1,0:T(8,128)S(1)} all-to-all(f32[16,8,128]{2,1,0:T(8,128)S(1)} %shard_map.106), channel_id=1, replica_groups=mesh['rows'=32,'cols'=16] {'cols'}, dimensions={0} | all-to-all | bytes 131072 | tf_op jit(solution)/shard_map/all_to_all | solution.py:375
  59.1 0.3 shard_map.107
  59.4 12.1 %all_to_all.17.attention_ref = bf16[32,8,128]{2,1,0:T(8,128)(2,1)S(1)} all-to-all(bf16[32,8,128]{2,1,0:T(8,128)(2,1)S(1)} %shard_map.107), channel_id=1, replica_groups=mesh['rows'=32,'cols'=16] {'rows'}, dimensions={0} | all-to-all | bytes 131072 | tf_op jit(solution)/shard_map/all_to_all | solution.py:377
  71.5 0.0 copy-done
  71.5 0.0 copy-done.1
  71.5 0.0 copy-done.2
  71.5 1.0 %shard_map.108 = (f32[100,256]{1,0:T(8,128)}, f32[100,256]{1,0:T(8,128)}) custom-call(bf16[32,8,128]{2,1,0:T(8,128)(2,1)S(1)} %all_to_all.17.attention_ref, bf16[256,256]{1,0:T(8,128)(2,1)S(1)} %copy-done.1, f32[100,256]{1,0:T(8,128)S(1)} %copy-done, f32[1,256]{1,0:T(1,128)S(1)} %bitcast.14), custom_call_target="tpu_custom_call" | custom-call | flops 10000000 | bytes 500000 | tf_op jit(solution)/shard_map/pallas_call | solution.py:335
  (5 shorter events, 0.0 us)
Async XLA Ops:
  1.6 10.2 %collective-permute-start = (bf16[16,256]{1,0:T(8,128)(2,1)S(1)}, bf16[16,256]{1,0:T(8,128)(2,1)S(1)}, u32[]{:S(2)}, u32[]{:S(2)}) collective-permute-start(bf16[16,256]{1,0:T(8,128)(2,1)S(1)} %get-tuple-element.29), channel_id=1, source_target_pairs={{1,2},{3,4},{5,6},{7,8},{9,10},{11,12},{13,14},{2,1},{4,3},{6,5},{... | collective-permute-start | bytes 24584 | tf_op jit(solution)/shard_map/ppermute | solution.py:352
  6.2 5.7 %collective-permute-start.1 = (bf16[16,256]{1,0:T(8,128)(2,1)S(1)}, bf16[16,256]{1,0:T(8,128)(2,1)S(1)}, u32[]{:S(2)}, u32[]{:S(2)}) collective-permute-start(bf16[16,256]{1,0:T(8,128)(2,1)S(1)} %get-tuple-element.30), channel_id=1, source_target_pairs={{0,1},{2,3},{4,5},{6,7},{8,9},{10,11},{12,13},{14,15},{1,0},{3,2},... | collective-permute-start | bytes 24584 | tf_op jit(solution)/shard_map/ppermute | solution.py:352
  11.9 7.8 %collective-permute-start.3 = (bf16[1,18,256]{2,1,0:T(8,128)(2,1)S(1)}, bf16[1,18,256]{2,1,0:T(8,128)(2,1)S(1)}, u32[]{:S(2)}, u32[]{:S(2)}) collective-permute-start(bf16[1,18,256]{2,1,0:T(8,128)(2,1)S(1)} %get-tuple-element.33), channel_id=1, source_target_pairs={{16,32},{48,64},{80,96},{112,128},{144,160},{176,192},{208,224},{2... | collective-permute-start | bytes 27656 | tf_op jit(solution)/shard_map/ppermute | solution.py:352
  12.5 7.1 %collective-permute-start.2 = (bf16[1,18,256]{2,1,0:T(8,128)(2,1)S(1)}, bf16[1,18,256]{2,1,0:T(8,128)(2,1)S(1)}, u32[]{:S(2)}, u32[]{:S(2)}) collective-permute-start(bf16[1,18,256]{2,1,0:T(8,128)(2,1)S(1)} %get-tuple-element.34), channel_id=1, source_target_pairs={{0,16},{32,48},{64,80},{96,112},{128,144},{160,176},{192,208},{224... | collective-permute-start | bytes 27656 | tf_op jit(solution)/shard_map/ppermute | solution.py:352
  19.7 51.8 %copy-start = (f32[100,256]{1,0:T(8,128)S(1)}, f32[100,256]{1,0:T(8,128)}, u32[]{:S(2)}) copy-start(f32[100,256]{1,0:T(8,128)} %queries_ref.1) | copy-start | bytes 307204
  19.7 51.8 %copy-start.1 = (bf16[256,256]{1,0:T(8,128)(2,1)S(1)}, bf16[256,256]{1,0:T(8,128)(2,1)}, u32[]{:S(2)}) copy-start(bf16[256,256]{1,0:T(8,128)(2,1)} %out_weight_ref.1) | copy-start | bytes 393220
  19.7 51.8 %copy-start.2 = (f32[256]{0:T(256)S(1)}, f32[256]{0:T(256)}, u32[]{:S(2)}) copy-start(f32[256]{0:T(256)} %param.14) | copy-start | bytes 3076
